TPU v7x, 32 devices: a whole 2x2x4 slice. The times are simulated.
32 devices in a mesh: case: 4 (over y, x), space: 8 (over z, core).
Axes of the slice: x: 2, y: 2, z: 4, core: 2. Of those that a mesh axis runs over, the one named last changes fastest.
Arguments:
- density: float32 [48, 32, 128], P('space', 'case'), may hold values from 0.3 to 1
- void_depth: int32 [48, 32], P('space', 'case'), may hold values from 0 to 32
- supports: int32 [4, 2], P('case'), may hold values from 1 to 12
- load_x: int32 [4], P('case'), may hold values from 0 to 40
- load_y: int32 [4], P('case'), may hold values from 0 to 24
- load_vectors: float32 [4, 3, 48], P('case'), may hold values from -4 to 4
Outputs:
- displacement: float32 [4, 3, 48, 32, 128], P('case', None, 'space')
- sensitivity: float32 [48, 32, 128], P('space', 'case')
All inputs are finite; a program needn't handle non-finite values.
Results may differ from a plain program's by a relative error of at most 0.0003.
Values sent between devices are 32-bit elements; how exact they have to be, the bound alone decides.
No kernel may reach another device: no remote copies, remote signals or barrier semaphores. Data moves between devices by JAX's collectives and lax.ppermute only.
A program may use at most 64 MiB of HBM per device.

v0:
```python
import math

import jax
import jax.numpy as jnp
from jax import lax
from jax.experimental import pallas as pl
from jax.experimental.pallas import tpu as pltpu
from jax.sharding import Mesh
from jax.sharding import PartitionSpec as P

SWEEPS = 3
LOADW = 8
EMIN = 0.001
LOWER = 0.06
UPPER = 3.0
PATCH = 4.0
SUB = 8
CORES = 2
HALO = SWEEPS + 1
EDGE = HALO - 1
PAD = 8

AXIAL = 1.5
PAIR = 0.625
FLAT = 0.5
FULL = 0.25 * (1.0 + 0.5 / 3.0)
CROSS2 = 0.125
CROSS3 = 0.125 / 3.0


def relaxations(count):
    middle = 0.5 * (UPPER + LOWER)
    radius = 0.5 * (UPPER - LOWER)
    return [
        1.0 / (middle + radius * math.cos(math.pi * (2 * index + 1) / (2 * count)))
        for index in range(count)
    ]


def both(pair):
    return pair[0] + pair[1], pair[0] - pair[1]


def plus(pair):
    return pair[0] + pair[1]


def minus(pair):
    return pair[0] - pair[1]


def span_of(cells):
    return CORES * cells + 2 * EDGE


def pack_kernel(
    density_ref, void_ref, supports_ref, load_x_ref, load_y_ref, vectors_ref, packed_ref
):
    copies, planes, band, depth = packed_ref.shape
    cells = planes - 1
    total_x = vectors_ref.shape[2]
    span = span_of(cells)
    first = lax.axis_index("column") * (CORES * cells) - EDGE
    z_of = lax.broadcasted_iota(jnp.int32, (band, depth), 1)
    level = z_of - depth // 2
    eye = lax.broadcasted_iota(jnp.int32, (band, band), 0) == lax.broadcasted_iota(
        jnp.int32, (band, band), 1
    )
    for i in range(cells):
        line = jnp.broadcast_to(void_ref[i : i + 1, :], (band, band)).astype(jnp.float32)
        column = jnp.sum(jnp.where(eye, line, 0.0), axis=1, keepdims=True)
        top = jnp.broadcast_to(column, (band, depth)).astype(jnp.int32)
        hollow = (level >= 0) & (level < top)
        solid = jnp.where(hollow, 0.0, density_ref[i])
        for copy in range(copies):
            packed_ref[copy, i] = solid
    lane = lax.broadcasted_iota(jnp.int32, (1, depth), 1)
    row = jnp.where(lane == 5 * span, load_y_ref[0].astype(jnp.float32), 0.0)
    for m in range(span):
        place = first + m
        inside = jnp.logical_and(place >= 0, place < total_x)
        where = jnp.clip(place, 0, total_x - 1)
        for k in range(3):
            value = jnp.where(inside, vectors_ref[0, k, where], 0.0)
            row = jnp.where(lane == k * span + m, value, row)
    place = first + lane - 3 * span
    pinned = (place < supports_ref[0, 0]) | (place >= total_x - supports_ref[0, 1])
    row = jnp.where((lane >= 3 * span) & (lane < 4 * span) & pinned, 1.0, row)
    place = first + lane - 4 * span
    loaded = (place >= load_x_ref[0]) & (place < load_x_ref[0] + LOADW)
    row = jnp.where((lane >= 4 * span) & (lane < 5 * span) & loaded, 1.0, row)
    for copy in range(copies):
        packed_ref[copy, cells] = jnp.broadcast_to(row, (band, depth))


def relax_kernel(
    chip_ref,
    halo_ref,
    field_ref,
    sensitivity_ref,
    natural,
    third_n,
    result_n,
    root_a,
    drive_a,
    push_a,
    inverse_a,
    shear_a,
    first_a,
    root_b,
    drive_b,
    push_b,
    inverse_b,
    shear_b,
    first_b,
    main_b,
    factor_b,
    second_b,
    squares_b,
    work_b,
):
    groups, cores, planes, band, depth = chip_ref.shape
    cells = planes - 1
    span = span_of(cells)
    rows = groups * band
    wide = cells + 2 * HALO
    core = lax.axis_index("core")
    case = lax.axis_index("case")
    chips = lax.axis_size("column")
    total_x = chips * CORES * cells
    first_plane = (lax.axis_index("column") * CORES + core) * cells
    shift = core * cells
    omegas = relaxations(SWEEPS)

    blank = jnp.zeros((PAD, depth), jnp.float32)
    tail = natural.shape[1] - PAD - rows
    for i in range(natural.shape[0]):
        natural[i, 0:PAD, :] = blank
        for at in range(PAD + rows, natural.shape[1], PAD):
            natural[i, at : at + PAD, :] = blank
    for k in range(3):
        for i in range(cells + 2):
            third_n[k, i, 0:PAD, :] = blank
            for at in range(PAD + rows, natural.shape[1], PAD):
                third_n[k, i, at : at + PAD, :] = blank
    for g in range(groups):
        lines = slice(PAD + g * band, PAD + (g + 1) * band)
        natural[0:HALO, lines, :] = halo_ref[g]
        for c in range(CORES):
            at = HALO + c * cells
            natural[at : at + cells, lines, :] = chip_ref[g, c, 0:cells]
        at = HALO + CORES * cells
        natural[at : at + HALO, lines, :] = halo_ref[g]

    tile = (1, SUB, depth)
    lane = lax.broadcasted_iota(jnp.int32, tile, 2)
    line = lax.broadcasted_iota(jnp.int32, tile, 1)
    not_first_z = (lane > 0).astype(jnp.float32)
    not_last_z = (lane < depth - 1).astype(jnp.float32)
    not_first_s = (line > 0).astype(jnp.float32)
    not_last_s = (line < SUB - 1).astype(jnp.float32)
    at_bottom = (lane == 0).astype(jnp.float32)

    def along_z(a):
        after = pltpu.roll(a, depth - 1, 2) * not_last_z
        before = pltpu.roll(a, 1, 2) * not_first_z
        return after, before

    def along_y(a, closed):
        fold = a.shape[0]
        after = pltpu.roll(a[0:1], SUB - 1, 1)
        before = pltpu.roll(a[fold - 1 : fold], 1, 1)
        if closed:
            after = after * not_last_s
            before = before * not_first_s
        return (
            jnp.concatenate([a[1:], after], axis=0),
            jnp.concatenate([before, a[:-1]], axis=0),
        )

    def inside_of(plane, margin):
        place = first_plane - margin + plane
        return jnp.logical_and(place >= 0, place < total_x).astype(jnp.float32)

    def lines_of(fold):
        shape = (fold, SUB, depth)
        return fold * lax.broadcasted_iota(jnp.int32, shape, 1) + lax.broadcasted_iota(
            jnp.int32, shape, 0
        )

    def case_values(which):
        plain = jnp.broadcast_to(chip_ref[which, 0, cells, 0:1, :], (SUB, depth))
        moved = pltpu.roll(plain, jnp.where(core == 0, 0, depth - cells), 1)

        def value(kind, j):
            at = kind * span + j
            return jnp.broadcast_to(moved[:, at : at + 1], (SUB, depth))[None]

        corner = jnp.broadcast_to(plain[:, 5 * span : 5 * span + 1], (SUB, depth))[None]
        return value, corner

    def patch_of(y_of, corner):
        y = y_of.astype(jnp.float32)
        high = lax.broadcasted_iota(jnp.int32, y_of.shape, 2) == depth - 1
        return jnp.where(high & (y >= corner) & (y < corner + LOADW), PATCH, 0.0)

    def stiffness(fold, start, keep_rows, root_s, drive_s, inv_s, factor_s):
        for i in range(wide):
            solid = jnp.stack(
                [natural[shift + i, pl.ds(start + t, SUB, stride=fold), :] for t in range(fold)]
            )
            stiff = EMIN + (1.0 - EMIN) * (solid * solid * solid)
            inv_root = lax.rsqrt(stiff)
            root = stiff * inv_root * inside_of(i, HALO)
            root_s[i] = root if keep_rows is None else root * keep_rows
            if 0 < i < wide - 1:
                drive_s[i - 1] = solid * inv_root
                inv_s[i - 1] = inv_root
            if factor_s is not None and HALO <= i < HALO + cells:
                ratio = solid * inv_root
                factor_s[i - HALO] = ((-1.5 * (1.0 - EMIN)) / groups) * (ratio * ratio)

    def tensor_parts(r, closed):
        zs, zd = both(along_z(r))
        ys, yd = both(along_y(r, closed))
        yszs, ydzs = both(along_y(zs, closed))
        yszd, ydzd = both(along_y(zd, closed))
        cross = ys + zs
        corner = PAIR * yszs
        here = [
            cross + FLAT * yszs,
            cross + 0.5 * ys + corner,
            cross + 0.5 * zs + corner,
            CROSS2 * ydzd,
        ]
        base = FULL * yszs + 0.5 * cross + r
        even = [
            base + 0.5 * r + 0.125 * cross,
            base + 0.125 * ys,
            base + 0.125 * zs,
            CROSS3 * ydzd,
        ]
        odd = [CROSS2 * yd + CROSS3 * ydzs, CROSS2 * zd + CROSS3 * yszd]
        return here, even, odd

    def tensor(closed, keep_rows, root_s, shear_s, inverse_s, main_s):
        older = None
        newer = None
        for i in range(wide):
            latest = tensor_parts(root_s[i], closed)
            if i >= 2:
                j = i - 2
                keep = inside_of(j, EDGE)
                if keep_rows is not None:
                    keep = keep * keep_rows
                total = [newer[0][k] + (latest[1][k] + older[1][k]) for k in range(4)]
                shear_s[0, j] = latest[2][0] - older[2][0]
                shear_s[1, j] = latest[2][1] - older[2][1]
                shear_s[2, j] = total[3]
                for k in range(3):
                    if main_s is not None and EDGE <= j < EDGE + cells:
                        main_s[k, j - EDGE] = total[k]
                    inverse_s[k, j] = keep / (total[k] + (1.0 - keep))
            older, newer = newer, latest

    def pushes(which, y_of, drive_s, inv_s, inverse_s, push_s):
        value, corner = case_values(which)
        patch = patch_of(y_of, corner)
        for j in range(wide - 2):
            free = 1.0 - value(3, j) * at_bottom
            push = (drive_s[j] + (value(4, j) * patch) * inv_s[j]) * free
            for k in range(3):
                push_s[k, j] = push * inverse_s[k, j] * value(k, j)
        return value

    def field_parts(w, closed):
        pair = [both(along_z(w[k])) for k in range(3)]
        zs = [pair[k][0] for k in range(3)]
        zd = [pair[k][1] for k in range(3)]
        ysx, ydx = both(along_y(w[0], closed))
        ysy, ydy = both(along_y(w[1], closed))
        ysz = plus(along_y(w[2], closed))
        yszsx, ydzsx = both(along_y(zs[0], closed))
        yszsy, ydzsy = both(along_y(zs[1], closed))
        yszsz = plus(along_y(zs[2], closed))
        yszdx = plus(along_y(zd[0], closed))
        ydzdy = minus(along_y(zd[1], closed))
        yszdz, ydzdz = both(along_y(zd[2], closed))
        here = [
            ysx + FLAT * yszsx + zs[0],
            AXIAL * ysy + PAIR * yszsy + zs[1] + CROSS2 * ydzdz,
            ysz + PAIR * yszsz + AXIAL * zs[2] + CROSS2 * ydzdy,
        ]
        even = [
            AXIAL * w[0] + PAIR * (zs[0] + ysx) + FULL * yszsx,
            w[1] + FLAT * zs[1] + PAIR * ysy + FULL * yszsy + CROSS3 * ydzdz,
            w[2] + PAIR * zs[2] + FLAT * ysz + FULL * yszsz + CROSS3 * ydzdy,
        ]
        odd = [
            CROSS2 * (ydy + zd[2]) + CROSS3 * (ydzsy + yszdz),
            CROSS2 * ydx + CROSS3 * ydzsx,
            CROSS2 * zd[0] + CROSS3 * yszdx,
        ]
        ahead = [even[k] + odd[k] for k in range(3)]
        behind = [even[k] - odd[k] for k in range(3)]
        return here, ahead, behind

    def sweep(closed, count, load, omega, value, store, root_s, push_s, inverse_s, shear_s):
        offset = (wide - count) // 2
        partial = None
        trail = None
        for i in range(count):
            r = root_s[i + offset]
            here, ahead, behind = field_parts([r * load(k, i) for k in range(3)], closed)
            if i >= 2:
                j = i - 1
                d = j + offset - 1
                free = 1.0 - value(3, d) * at_bottom
                old = [load(k, j) for k in range(3)]
                shear = [shear_s[k, d] for k in range(3)]
                rest = [
                    shear[0] * old[1] + shear[1] * old[2],
                    shear[0] * old[0] + shear[2] * old[2],
                    shear[1] * old[0] + shear[2] * old[1],
                ]
                for k in range(3):
                    pull = (partial[k] + ahead[k] - rest[k]) * (inverse_s[k, d] * free)
                    store(k, j - 1, (1.0 - omega) * old[k] + omega * (push_s[k, d] + pull))
            if i >= 1:
                partial = [here[k] + trail[k] for k in range(3)]
            trail = behind

    fold = rows // SUB
    inv_a = first_a.at[0]
    stiffness(fold, PAD, None, root_a, drive_a, inv_a, None)
    tensor(True, None, root_a, shear_a, inverse_a, None)
    value = pushes(case, lines_of(fold), drive_a, inv_a, inverse_a, push_a)

    def store_first_a(k, i, new):
        first_a[k, i] = new

    def store_third_a(k, i, new):
        for t in range(fold):
            third_n[k, i, pl.ds(PAD + t, SUB, stride=fold), :] = new[t]
            if 1 <= i <= cells:
                field_ref[k, i - 1, pl.ds(t, SUB, stride=fold), :] = new[t]

    arrays = (root_a, push_a, inverse_a, shear_a)
    sweep(
        True, wide - 2, lambda k, i: omegas[0] * push_a[k, i], omegas[1], value, store_first_a, *arrays
    )
    sweep(True, wide - 4, lambda k, i: first_a[k, i], omegas[2], value, store_third_a, *arrays)

    fold_b = result_n.shape[1] // SUB
    top = case * band - HALO
    y_of = top + lines_of(fold_b)
    keep_rows = ((y_of >= 0) & (y_of < rows)).astype(jnp.float32)
    inv_b = work_b.at[pl.ds(0, wide - 2)]
    stiffness(fold_b, PAD + top, keep_rows, root_b, drive_b, inv_b, factor_b)
    tensor(False, keep_rows, root_b, shear_b, inverse_b, main_b)
    gathered = work_b.at[pl.ds(wide - 2, cells)]
    empty = jnp.zeros((fold_b, SUB, depth), jnp.float32)
    for i in range(cells + 2):
        for n in range(6):
            squares_b[n, i] = empty
    for i in range(cells):
        gathered[i] = empty

    def store_first_b(k, i, new):
        first_b[k, i] = new

    def store_second_b(k, i, new):
        second_b[k, i] = new

    @pl.loop(0, groups)
    def add_case(other):
        @pl.when(other == 0)
        def take_own():
            for k in range(3):
                for i in range(cells + 2):
                    second_b[k, i] = jnp.stack(
                        [
                            third_n[k, i, pl.ds(PAD + top + t, SUB, stride=fold_b), :]
                            for t in range(fold_b)
                        ]
                    )

        @pl.when(other > 0)
        def relax_other():
            which = lax.rem(case + other, groups)
            value = pushes(which, y_of, drive_b, inv_b, inverse_b, push_b)
            arrays = (root_b, push_b, inverse_b, shear_b)
            sweep(
                False,
                wide - 2,
                lambda k, i: omegas[0] * push_b[k, i],
                omegas[1],
                value,
                store_first_b,
                *arrays,
            )
            sweep(
                False, wide - 4, lambda k, i: first_b[k, i], omegas[2], value, store_second_b, *arrays
            )

        partial = None
        trail = None
        for i in range(cells + 2):
            r = root_b[i + EDGE]
            v = [second_b[k, i] for k in range(3)]
            w = [r * v[k] for k in range(3)]
            for n, (a, b) in enumerate(((0, 0), (1, 1), (2, 2), (0, 1), (0, 2), (1, 2))):
                squares_b[n, i] += w[a] * v[b]
            here, ahead, behind = field_parts(w, False)
            if i >= 2:
                old = [second_b[k, i - 1] for k in range(3)]
                dot = [old[k] * (partial[k] + ahead[k]) for k in range(3)]
                gathered[i - 2] += dot[0] + dot[1] + dot[2]
            if i >= 1:
                partial = [here[k] + trail[k] for k in range(3)]
            trail = behind

    def square_parts(q):
        qxx, qyy, qzz, qxy, qxz, qyz = q
        s = qxx + qyy + qzz
        zs_s = plus(along_z(s))
        zs_x = plus(along_z(qxx))
        zs_z = plus(along_z(qzz))
        zs_xy = plus(along_z(qxy))
        zd_yz = minus(along_z(qyz))
        zd_xz = minus(along_z(qxz))
        twist = minus(along_y(zd_yz, False))
        half = 0.5 * zs_s + 0.125 * zs_z
        here = (
            zs_s
            + 0.5 * zs_z
            + plus(along_y(s + 0.5 * qyy + (PAIR * zs_s - 0.125 * zs_x), False))
            + 0.25 * twist
        )
        even = (
            s
            + 0.5 * qxx
            + half
            + 0.125 * zs_x
            + plus(along_y(0.5 * s + 0.125 * (qxx + qyy) + FULL * zs_s, False))
            + (1.0 / 12.0) * twist
        )
        odd = (
            minus(along_y(0.25 * qxy + (1.0 / 12.0) * zs_xy, False))
            + 0.25 * zd_xz
            + plus(along_y((1.0 / 12.0) * zd_xz, False))
        )
        return here, even + odd, even - odd

    partial = None
    trail = None
    for i in range(cells + 2):
        here, ahead, behind = square_parts([squares_b[n, i] for n in range(6)])
        if i >= 2:
            j = i - 2
            q = [squares_b[n, i - 1] for n in range(6)]
            d = j + EDGE
            held = main_b[0, j] * q[0] + main_b[1, j] * q[1] + main_b[2, j] * q[2]
            mixed = shear_b[0, d] * q[3] + shear_b[1, d] * q[4] + shear_b[2, d] * q[5]
            rest = partial + ahead - 2.0 * gathered[j]
            total = held + 2.0 * mixed + root_b[d + 1] * rest
            total = total * factor_b[j]
            for t in range(fold_b):
                result_n[j, pl.ds(t, SUB, stride=fold_b), :] = total[t]
        if i >= 1:
            partial = here + trail
        trail = behind
    sensitivity_ref[...] = result_n[:, HALO : HALO + band, :]


def on_vmem():
    return pl.BlockSpec(memory_space=pltpu.VMEM)


def on_smem():
    return pl.BlockSpec(memory_space=pltpu.SMEM)


def packed(density, void_depth, supports, load_x, load_y, load_vectors):
    cells, band, depth = density.shape
    copies = lax.axis_size("case") * CORES
    return pl.pallas_call(
        pack_kernel,
        out_shape=jax.ShapeDtypeStruct((copies, cells + 1, band, depth), jnp.float32),
        in_specs=[on_vmem()] * 2 + [on_smem()] * 4,
        out_specs=on_vmem(),
    )(density, void_depth, supports, load_x, load_y, load_vectors)


def relaxed(chip, halo):
    groups, cores, planes, band, depth = chip.shape
    cells = planes - 1
    rows = groups * band
    wide = cells + 2 * HALO
    fold = rows // SUB
    fold_b = -(-(band + 2 * HALO) // SUB)
    tall = PAD + rows + fold_b * SUB

    def area(*lead):
        return pltpu.VMEM((*lead, fold, SUB, depth), jnp.float32)

    def window(*lead):
        return pltpu.VMEM((*lead, fold_b, SUB, depth), jnp.float32)

    return pl.pallas_call(
        relax_kernel,
        out_shape=(
            jax.ShapeDtypeStruct((3, cells, rows, depth), jnp.float32),
            jax.ShapeDtypeStruct((cells, band, depth), jnp.float32),
        ),
        in_specs=[on_vmem()] * 2,
        out_specs=(on_vmem(), on_vmem()),
        scratch_shapes=[
            pltpu.VMEM((CORES * cells + 2 * HALO, tall, depth), jnp.float32),
            pltpu.VMEM((3, cells + 2, tall, depth), jnp.float32),
            pltpu.VMEM((cells, fold_b * SUB, depth), jnp.float32),
            area(wide),
            area(wide - 2),
            area(3, wide - 2),
            area(3, wide - 2),
            area(3, wide - 2),
            area(3, wide - 2),
            window(wide),
            window(wide - 2),
            window(3, wide - 2),
            window(3, wide - 2),
            window(3, wide - 2),
            window(3, wide - 4),
            window(3, cells),
            window(cells),
            window(3, cells + 2),
            window(6, cells + 2),
            window(wide - 2 + cells),
        ],
        compiler_params=pltpu.CompilerParams(vmem_limit_bytes=32 * 1024 * 1024),
    )(chip, halo)


def shards(density, void_depth, supports, load_x, load_y, load_vectors):
    cells, band, depth = density.shape
    groups = lax.axis_size("case")
    slabs = lax.axis_size("column") * CORES
    mine = packed(density, void_depth, supports, load_x, load_y, load_vectors)
    chip = lax.all_to_all(mine, ("case", "core"), split_axis=0, concat_axis=0, tiled=True)
    chip = chip.reshape(groups, CORES, cells + 1, band, depth)
    low = chip[:, 0, :HALO]
    high = chip[:, 1, cells - HALO : cells]
    near = jnp.where(lax.axis_index("core") == 0, low, high)
    pairs = [(i, i + 1) for i in range(1, slabs - 1, 2)]
    pairs += [(j, i) for i, j in pairs]
    halo = lax.ppermute(near, ("column", "core"), pairs)
    field, sensitivity = relaxed(chip, halo)
    return (field[None], sensitivity)


def solution(mesh):
    groups, slabs = mesh.devices.shape
    chips = Mesh(mesh.devices.reshape(groups, slabs // CORES, CORES), ("case", "column", "core"))
    space = ("column", "core")
    return jax.shard_map(
        shards,
        mesh=chips,
        in_specs=(
            P(space, "case", None),
            P(space, "case"),
            P("case", None),
            P("case"),
            P("case"),
            P("case", None, None),
        ),
        out_specs=(P("case", None, space, None, None), P(space, "case", None)),
        check_vma=False,
    )
```

profile of v0, /device:TPU:1, one launch (start us, length us, event | category | flops | bytes accessed | tf_op | source)
XLA Modules:
  0.0 28.3 jit_solution(803520322004168868)
XLA Ops:
  0.6 0.0 copy-start
  1.9 0.0 copy-done
  2.0 0.6 %copy.10.vectors_ref = f32[1,3,48]{2,1,0:T(4,128)} copy(f32[1,3,48]{2,0,1:T(1,128)S(1)} %copy-done) | data formatting | bytes 1152 | tf_op args[5]
  2.5 1.6 %shard_map.77 = f32[8,7,8,128]{3,2,1,0:T(8,128)} custom-call(f32[6,8,128]{2,1,0:T(8,128)} %density_ref.1, s32[6,8]{1,0:T(8,128)} %void_ref.1, s32[1,2]{1,0:T(1,128)} %supports_ref.1, s32[1]{0:T(128)S(6)} %copy.15.load_x_ref, s32[1]{0:T(128)S(6)} %copy.16.load_y_ref, f32[1,3,48]{2,1,0:T(4,128)} %copy.10.vectors_ref), custom_call_target="tpu_custom_call" | custom-call | tf_op jit(solution)/shard_map/pallas_call | solution.py:487
  4.2 5.2 %all-to-all-start = ((f32[8,7,8,128]{3,2,1,0:T(8,128)}), f32[8,7,8,128]{3,2,1,0:T(8,128)S(1)}, u32[]{:S(2)}, u32[]{:S(2)}) async-start(f32[8,7,8,128]{3,2,1,0:T(8,128)} %shard_map.77), calls=%async_computation | async-start | bytes 458752 | tf_op jit(solution)/shard_map/all_to_all | solution.py:549
  9.4 5.4 %all-to-all-done = f32[8,7,8,128]{3,2,1,0:T(8,128)S(1)} async-done(((f32[8,7,8,128]{3,2,1,0:T(8,128)}), f32[8,7,8,128]{3,2,1,0:T(8,128)S(1)}, u32[]{:S(2)}, u32[]{:S(2)}) %all-to-all-start) | async-done | bytes 229408 | tf_op jit(solution)/shard_map/all_to_all | solution.py:549
  14.8 4.2 %collective-permute-start = (f32[4,4,8,128]{3,2,1,0:T(8,128)S(1)}, f32[4,4,8,128]{3,2,1,0:T(8,128)S(1)}, u32[]{:S(2)}, u32[]{:S(2)}) collective-permute-start(f32[4,4,8,128]{3,2,1,0:T(8,128)S(1)} %fusion.1), channel_id=1, source_target_pairs={{1,2},{3,4},{5,6},{2,1},{4,3},{6,5},{9,10},{11,12},{13,14},{10,9},... | collective-permute-start | bytes 196616 | tf_op jit(solution)/shard_map/ppermute | solution.py:556
  19.1 1.9 %collective-permute-done.halo_ref = f32[4,4,8,128]{3,2,1,0:T(8,128)S(1)} collective-permute-done((f32[4,4,8,128]{3,2,1,0:T(8,128)S(1)}, f32[4,4,8,128]{3,2,1,0:T(8,128)S(1)}, u32[]{:S(2)}, u32[]{:S(2)}) %collective-permute-start) | collective-permute-done | bytes 65568 | tf_op jit(solution)/shard_map/ppermute | solution.py:556
  21.0 7.3 %shard_map.78 = (f32[3,6,32,128]{3,2,1,0:T(8,128)}, f32[6,8,128]{2,1,0:T(8,128)}) custom-call(f32[4,2,7,8,128]{4,3,2,1,0:T(8,128)S(1)} %bitcast.15, f32[4,4,8,128]{3,2,1,0:T(8,128)S(1)} %collective-permute-done.halo_ref), custom_call_target="tpu_custom_call" | custom-call | tf_op jit(solution)/shard_map/pallas_call | solution.py:510
  (1 shorter events, 0.0 us)
Async XLA Ops:
  0.6 1.3 %copy-start = (f32[1,3,48]{2,0,1:T(1,128)S(1)}, f32[1,3,48]{2,0,1:T(1,128)}, u32[]{:S(2)}) copy-start(f32[1,3,48]{2,0,1:T(1,128)} %param.11) | copy-start | bytes 1732
  4.2 10.7 %all-to-all-start = ((f32[8,7,8,128]{3,2,1,0:T(8,128)}), f32[8,7,8,128]{3,2,1,0:T(8,128)S(1)}, u32[]{:S(2)}, u32[]{:S(2)}) async-start(f32[8,7,8,128]{3,2,1,0:T(8,128)} %shard_map.77), calls=%async_computation | async-start | bytes 458752 | tf_op jit(solution)/shard_map/all_to_all | solution.py:549
  14.8 6.2 %collective-permute-start = (f32[4,4,8,128]{3,2,1,0:T(8,128)S(1)}, f32[4,4,8,128]{3,2,1,0:T(8,128)S(1)}, u32[]{:S(2)}, u32[]{:S(2)}) collective-permute-start(f32[4,4,8,128]{3,2,1,0:T(8,128)S(1)} %fusion.1), channel_id=1, source_target_pairs={{1,2},{3,4},{5,6},{2,1},{4,3},{6,5},{9,10},{11,12},{13,14},{10,9},... | collective-permute-start | bytes 196616 | tf_op jit(solution)/shard_map/ppermute | solution.py:556
where the time goes:
time: 28.6 us; the launch traced here: 28.3 us
  starting transfers between devices  9.46 us (33%)
  Pallas kernels  8.88 us (31%)
  waiting for transfers between devices  7.37 us (26%)
  between operations  1.96 us (7%)
  local copies, waits for them, and re-layouts  0.58 us (2%)
    pallas_call x1, Pallas kernels, relaxed(): pl.pallas_call(relax_kernel, out_shape=(jax.ShapeDtypeStruct((3, cells, r...  7.25 us
    all_to_all x1, waiting for transfers between devices, shards(): lax.all_to_all(mine, ('case', 'core'), split_axis=0, concat_axis=0, tiled...  5.44 us
    all_to_all x1, starting transfers between devices, shards(): lax.all_to_all(mine, ('case', 'core'), split_axis=0, concat_axis=0, tiled...  5.22 us
    ppermute x1, starting transfers between devices, shards(): halo = lax.ppermute(near, ('column', 'core'), pairs)  4.24 us
    ppermute x1, waiting for transfers between devices, shards(): halo = lax.ppermute(near, ('column', 'core'), pairs)  1.93 us
    pallas_call x1, Pallas kernels, packed(): pl.pallas_call(pack_kernel, out_shape=jax.ShapeDtypeStruct((copies, cells...  1.63 us
    unnamed x3, local copies, waits for them, and re-layouts  0.58 us
  transfers between devices with their start and end apart: 2, of which 2 were waited for; matrix products, arithmetic and copies ran while one was open for 0% of the time, Pallas kernels for 0%

commit v1 on v0

--- a/solution.py
+++ b/solution.py
@@ -54,8 +54,34 @@
 
 
 def pack_kernel(
-    density_ref, void_ref, supports_ref, load_x_ref, load_y_ref, vectors_ref, packed_ref
+    density_in,
+    void_in,
+    supports_in,
+    vectors_in,
+    load_x_ref,
+    load_y_ref,
+    packed_ref,
+    density_ref,
+    void_ref,
+    supports_ref,
+    vectors_ref,
+    arrived,
 ):
+    fetches = [
+        pltpu.make_async_copy(source, target, arrived.at[n])
+        for n, (source, target) in enumerate(
+            (
+                (supports_in, supports_ref),
+                (vectors_in, vectors_ref),
+                (void_in, void_ref),
+                (density_in, density_ref),
+            )
+        )
+    ]
+    for fetch in fetches:
+        fetch.start()
+    for fetch in fetches:
+        fetch.wait()
     copies, planes, band, depth = packed_ref.shape
     cells = planes - 1
     total_x = vectors_ref.shape[2]
@@ -81,7 +107,7 @@
         inside = jnp.logical_and(place >= 0, place < total_x)
         where = jnp.clip(place, 0, total_x - 1)
         for k in range(3):
-            value = jnp.where(inside, vectors_ref[0, k, where], 0.0)
+            value = jnp.where(inside, vectors_ref[k, 0, where], 0.0)
             row = jnp.where(lane == k * span + m, value, row)
     place = first + lane - 3 * span
     pinned = (place < supports_ref[0, 0]) | (place >= total_x - supports_ref[0, 1])
@@ -484,12 +510,27 @@
 def packed(density, void_depth, supports, load_x, load_y, load_vectors):
     cells, band, depth = density.shape
     copies = lax.axis_size("case") * CORES
+    vectors = load_vectors.transpose(1, 0, 2)
     return pl.pallas_call(
         pack_kernel,
-        out_shape=jax.ShapeDtypeStruct((copies, cells + 1, band, depth), jnp.float32),
-        in_specs=[on_vmem()] * 2 + [on_smem()] * 4,
+        out_shape=pltpu.VMEM((copies, cells + 1, band, depth), jnp.float32),
+        in_specs=[pl.BlockSpec(memory_space=pltpu.HBM)] * 4 + [on_smem()] * 2,
         out_specs=on_vmem(),
-    )(density, void_depth, supports, load_x, load_y, load_vectors)
+        scratch_shapes=[
+            pltpu.VMEM(density.shape, jnp.float32),
+            pltpu.VMEM(void_depth.shape, jnp.int32),
+            pltpu.SMEM(supports.shape, jnp.int32),
+            pltpu.SMEM(vectors.shape, jnp.float32),
+            pltpu.SemaphoreType.DMA((4,)),
+        ],
+    )(
+        *(
+            pltpu.with_memory_space_constraint(array, pltpu.HBM)
+            for array in (density, void_depth, supports, vectors)
+        ),
+        load_x,
+        load_y,
+    )
 
 
 def relaxed(chip, halo):

time: 28.6 us -> 27.9 us (0.976)
  local copies, waits for them, and re-layouts: 0.58 us -> 0 us
    unnamed x3 -> x0, local copies, waits for them, and re-layouts: 0.58 us -> none
where the time goes in v1:
time: 27.9 us; the launch traced here: 27.6 us
  starting transfers between devices  9.48 us (34%)
  Pallas kernels  8.84 us (32%)
  waiting for transfers between devices  7.37 us (26%)
  between operations  1.94 us (7%)
    pallas_call x1, Pallas kernels, relaxed(): pl.pallas_call(relax_kernel, out_shape=(jax.ShapeDtypeStruct((3, cells, r...  7.25 us
    all_to_all x1, waiting for transfers between devices, shards(): lax.all_to_all(mine, ('case', 'core'), split_axis=0, concat_axis=0, tiled...  5.44 us
    all_to_all x1, starting transfers between devices, shards(): lax.all_to_all(mine, ('case', 'core'), split_axis=0, concat_axis=0, tiled...  5.24 us
    ppermute x1, starting transfers between devices, shards(): halo = lax.ppermute(near, ('column', 'core'), pairs)  4.24 us
    ppermute x1, waiting for transfers between devices, shards(): halo = lax.ppermute(near, ('column', 'core'), pairs)  1.93 us
    pallas_call x1, Pallas kernels, packed(): pl.pallas_call(pack_kernel, out_shape=pltpu.VMEM((copies, cells + 1, band...  1.59 us
  transfers between devices with their start and end apart: 2, of which 2 were waited for; matrix products, arithmetic and copies ran while one was open for 0% of the time, Pallas kernels for 0%

profile of v1, /device:TPU:1, one launch (start us, length us, event | category | flops | bytes accessed | tf_op | source)
XLA Modules:
  0.0 27.6 jit_solution(13589703480411548246)
XLA Ops:
  1.9 1.6 %shard_map.77 = f32[8,7,8,128]{3,2,1,0:T(8,128)} custom-call(f32[6,8,128]{2,1,0:T(8,128)} %density_in.1, s32[6,8]{1,0:T(8,128)} %void_in.1, s32[1,2]{1,0:T(1,128)} %supports_in.1, f32[3,1,48]{2,1,0:T(1,128)} %bitcast.17, s32[1]{0:T(128)S(6)} %copy.13.load_x_ref, s32[1]{0:T(128)S(6)} %copy.14.load_y_ref), custom_call_target="tpu_custom_call" | custom-call | tf_op jit(solution)/shard_map/pallas_call | solution.py:514
  3.5 5.2 %all-to-all-start = ((f32[8,7,8,128]{3,2,1,0:T(8,128)}), f32[8,7,8,128]{3,2,1,0:T(8,128)S(1)}, u32[]{:S(2)}, u32[]{:S(2)}) async-start(f32[8,7,8,128]{3,2,1,0:T(8,128)} %shard_map.77), calls=%async_computation | async-start | bytes 458752 | tf_op jit(solution)/shard_map/all_to_all | solution.py:590
  8.8 5.4 %all-to-all-done = f32[8,7,8,128]{3,2,1,0:T(8,128)S(1)} async-done(((f32[8,7,8,128]{3,2,1,0:T(8,128)}), f32[8,7,8,128]{3,2,1,0:T(8,128)S(1)}, u32[]{:S(2)}, u32[]{:S(2)}) %all-to-all-start) | async-done | bytes 229408 | tf_op jit(solution)/shard_map/all_to_all | solution.py:590
  14.2 4.2 %collective-permute-start = (f32[4,4,8,128]{3,2,1,0:T(8,128)S(1)}, f32[4,4,8,128]{3,2,1,0:T(8,128)S(1)}, u32[]{:S(2)}, u32[]{:S(2)}) collective-permute-start(f32[4,4,8,128]{3,2,1,0:T(8,128)S(1)} %fusion.1), channel_id=1, source_target_pairs={{1,2},{3,4},{5,6},{2,1},{4,3},{6,5},{9,10},{11,12},{13,14},{10,9},... | collective-permute-start | bytes 196616 | tf_op jit(solution)/shard_map/ppermute | solution.py:597
  18.5 1.9 %collective-permute-done.halo_ref = f32[4,4,8,128]{3,2,1,0:T(8,128)S(1)} collective-permute-done((f32[4,4,8,128]{3,2,1,0:T(8,128)S(1)}, f32[4,4,8,128]{3,2,1,0:T(8,128)S(1)}, u32[]{:S(2)}, u32[]{:S(2)}) %collective-permute-start) | collective-permute-done | bytes 65568 | tf_op jit(solution)/shard_map/ppermute | solution.py:597
  20.4 7.3 %shard_map.78 = (f32[3,6,32,128]{3,2,1,0:T(8,128)}, f32[6,8,128]{2,1,0:T(8,128)}) custom-call(f32[4,2,7,8,128]{4,3,2,1,0:T(8,128)S(1)} %bitcast.16, f32[4,4,8,128]{3,2,1,0:T(8,128)S(1)} %collective-permute-done.halo_ref), custom_call_target="tpu_custom_call" | custom-call | tf_op jit(solution)/shard_map/pallas_call | solution.py:551
  (1 shorter events, 0.0 us)
Async XLA Ops:
  3.5 10.7 %all-to-all-start = ((f32[8,7,8,128]{3,2,1,0:T(8,128)}), f32[8,7,8,128]{3,2,1,0:T(8,128)S(1)}, u32[]{:S(2)}, u32[]{:S(2)}) async-start(f32[8,7,8,128]{3,2,1,0:T(8,128)} %shard_map.77), calls=%async_computation | async-start | bytes 458752 | tf_op jit(solution)/shard_map/all_to_all | solution.py:590
  14.2 6.2 %collective-permute-start = (f32[4,4,8,128]{3,2,1,0:T(8,128)S(1)}, f32[4,4,8,128]{3,2,1,0:T(8,128)S(1)}, u32[]{:S(2)}, u32[]{:S(2)}) collective-permute-start(f32[4,4,8,128]{3,2,1,0:T(8,128)S(1)} %fusion.1), channel_id=1, source_target_pairs={{1,2},{3,4},{5,6},{2,1},{4,3},{6,5},{9,10},{11,12},{13,14},{10,9},... | collective-permute-start | bytes 196616 | tf_op jit(solution)/shard_map/ppermute | solution.py:597

commit v2 on v0

--- a/solution.py
+++ b/solution.py
@@ -5,7 +5,6 @@
 from jax import lax
 from jax.experimental import pallas as pl
 from jax.experimental.pallas import tpu as pltpu
-from jax.sharding import Mesh
 from jax.sharding import PartitionSpec as P
 
 SWEEPS = 3
@@ -15,7 +14,6 @@
 UPPER = 3.0
 PATCH = 4.0
 SUB = 8
-CORES = 2
 HALO = SWEEPS + 1
 EDGE = HALO - 1
 PAD = 8
@@ -50,30 +48,26 @@
 
 
 def span_of(cells):
-    return CORES * cells + 2 * EDGE
-
-
-def pack_kernel(
-    density_ref, void_ref, supports_ref, load_x_ref, load_y_ref, vectors_ref, packed_ref
+    return cells + 2 * EDGE
+
+
+def settings_kernel(
+    supports_in, vectors_in, load_x_ref, load_y_ref, row_ref, supports_ref, vectors_ref, arrived
 ):
-    copies, planes, band, depth = packed_ref.shape
-    cells = planes - 1
+    fetches = [
+        pltpu.make_async_copy(supports_in, supports_ref, arrived.at[0]),
+        pltpu.make_async_copy(vectors_in, vectors_ref, arrived.at[1]),
+    ]
+    for fetch in fetches:
+        fetch.start()
+    for fetch in fetches:
+        fetch.wait()
+    slabs = lax.axis_size("space")
+    band, depth = row_ref.shape[1:]
     total_x = vectors_ref.shape[2]
+    cells = total_x // slabs
     span = span_of(cells)
-    first = lax.axis_index("column") * (CORES * cells) - EDGE
-    z_of = lax.broadcasted_iota(jnp.int32, (band, depth), 1)
-    level = z_of - depth // 2
-    eye = lax.broadcasted_iota(jnp.int32, (band, band), 0) == lax.broadcasted_iota(
-        jnp.int32, (band, band), 1
-    )
-    for i in range(cells):
-        line = jnp.broadcast_to(void_ref[i : i + 1, :], (band, band)).astype(jnp.float32)
-        column = jnp.sum(jnp.where(eye, line, 0.0), axis=1, keepdims=True)
-        top = jnp.broadcast_to(column, (band, depth)).astype(jnp.int32)
-        hollow = (level >= 0) & (level < top)
-        solid = jnp.where(hollow, 0.0, density_ref[i])
-        for copy in range(copies):
-            packed_ref[copy, i] = solid
+    first = lax.axis_index("space") * cells - EDGE
     lane = lax.broadcasted_iota(jnp.int32, (1, depth), 1)
     row = jnp.where(lane == 5 * span, load_y_ref[0].astype(jnp.float32), 0.0)
     for m in range(span):
@@ -81,7 +75,7 @@
         inside = jnp.logical_and(place >= 0, place < total_x)
         where = jnp.clip(place, 0, total_x - 1)
         for k in range(3):
-            value = jnp.where(inside, vectors_ref[0, k, where], 0.0)
+            value = jnp.where(inside, vectors_ref[k, 0, where], 0.0)
             row = jnp.where(lane == k * span + m, value, row)
     place = first + lane - 3 * span
     pinned = (place < supports_ref[0, 0]) | (place >= total_x - supports_ref[0, 1])
@@ -89,13 +83,11 @@
     place = first + lane - 4 * span
     loaded = (place >= load_x_ref[0]) & (place < load_x_ref[0] + LOADW)
     row = jnp.where((lane >= 4 * span) & (lane < 5 * span) & loaded, 1.0, row)
-    for copy in range(copies):
-        packed_ref[copy, cells] = jnp.broadcast_to(row, (band, depth))
+    row_ref[0] = jnp.broadcast_to(row, (band, depth))
 
 
 def relax_kernel(
-    chip_ref,
-    halo_ref,
+    bands_ref,
     field_ref,
     sensitivity_ref,
     natural,
@@ -119,22 +111,18 @@
     squares_b,
     work_b,
 ):
-    groups, cores, planes, band, depth = chip_ref.shape
-    cells = planes - 1
+    groups, planes, band, depth = bands_ref.shape
+    wide = planes - 1
+    cells = wide - 2 * HALO
     span = span_of(cells)
     rows = groups * band
-    wide = cells + 2 * HALO
-    core = lax.axis_index("core")
     case = lax.axis_index("case")
-    chips = lax.axis_size("column")
-    total_x = chips * CORES * cells
-    first_plane = (lax.axis_index("column") * CORES + core) * cells
-    shift = core * cells
+    total_x = lax.axis_size("space") * cells
+    first_plane = lax.axis_index("space") * cells
     omegas = relaxations(SWEEPS)
 
     blank = jnp.zeros((PAD, depth), jnp.float32)
-    tail = natural.shape[1] - PAD - rows
-    for i in range(natural.shape[0]):
+    for i in range(wide):
         natural[i, 0:PAD, :] = blank
         for at in range(PAD + rows, natural.shape[1], PAD):
             natural[i, at : at + PAD, :] = blank
@@ -144,13 +132,7 @@
             for at in range(PAD + rows, natural.shape[1], PAD):
                 third_n[k, i, at : at + PAD, :] = blank
     for g in range(groups):
-        lines = slice(PAD + g * band, PAD + (g + 1) * band)
-        natural[0:HALO, lines, :] = halo_ref[g]
-        for c in range(CORES):
-            at = HALO + c * cells
-            natural[at : at + cells, lines, :] = chip_ref[g, c, 0:cells]
-        at = HALO + CORES * cells
-        natural[at : at + HALO, lines, :] = halo_ref[g]
+        natural[:, PAD + g * band : PAD + (g + 1) * band, :] = bands_ref[g, 0:wide]
 
     tile = (1, SUB, depth)
     lane = lax.broadcasted_iota(jnp.int32, tile, 2)
@@ -189,12 +171,11 @@
         )
 
     def case_values(which):
-        plain = jnp.broadcast_to(chip_ref[which, 0, cells, 0:1, :], (SUB, depth))
-        moved = pltpu.roll(plain, jnp.where(core == 0, 0, depth - cells), 1)
+        plain = jnp.broadcast_to(bands_ref[which, wide, 0:1, :], (SUB, depth))
 
         def value(kind, j):
             at = kind * span + j
-            return jnp.broadcast_to(moved[:, at : at + 1], (SUB, depth))[None]
+            return jnp.broadcast_to(plain[:, at : at + 1], (SUB, depth))[None]
 
         corner = jnp.broadcast_to(plain[:, 5 * span : 5 * span + 1], (SUB, depth))[None]
         return value, corner
@@ -207,7 +188,7 @@
     def stiffness(fold, start, keep_rows, root_s, drive_s, inv_s, factor_s):
         for i in range(wide):
             solid = jnp.stack(
-                [natural[shift + i, pl.ds(start + t, SUB, stride=fold), :] for t in range(fold)]
+                [natural[i, pl.ds(start + t, SUB, stride=fold), :] for t in range(fold)]
             )
             stiff = EMIN + (1.0 - EMIN) * (solid * solid * solid)
             inv_root = lax.rsqrt(stiff)
@@ -481,22 +462,30 @@
     return pl.BlockSpec(memory_space=pltpu.SMEM)
 
 
-def packed(density, void_depth, supports, load_x, load_y, load_vectors):
-    cells, band, depth = density.shape
-    copies = lax.axis_size("case") * CORES
+def settings(band, depth, supports, load_x, load_y, load_vectors):
+    vectors = load_vectors.transpose(1, 0, 2)
     return pl.pallas_call(
-        pack_kernel,
-        out_shape=jax.ShapeDtypeStruct((copies, cells + 1, band, depth), jnp.float32),
-        in_specs=[on_vmem()] * 2 + [on_smem()] * 4,
+        settings_kernel,
+        out_shape=jax.ShapeDtypeStruct((1, band, depth), jnp.float32),
+        in_specs=[pl.BlockSpec(memory_space=pltpu.HBM)] * 2 + [on_smem()] * 2,
         out_specs=on_vmem(),
-    )(density, void_depth, supports, load_x, load_y, load_vectors)
-
-
-def relaxed(chip, halo):
-    groups, cores, planes, band, depth = chip.shape
-    cells = planes - 1
+        scratch_shapes=[
+            pltpu.SMEM(supports.shape, jnp.int32),
+            pltpu.SMEM(vectors.shape, jnp.float32),
+            pltpu.SemaphoreType.DMA((2,)),
+        ],
+    )(
+        *(pltpu.with_memory_space_constraint(array, pltpu.HBM) for array in (supports, vectors)),
+        load_x,
+        load_y,
+    )
+
+
+def relaxed(bands):
+    groups, planes, band, depth = bands.shape
+    wide = planes - 1
+    cells = wide - 2 * HALO
     rows = groups * band
-    wide = cells + 2 * HALO
     fold = rows // SUB
     fold_b = -(-(band + 2 * HALO) // SUB)
     tall = PAD + rows + fold_b * SUB
@@ -513,10 +502,10 @@
             jax.ShapeDtypeStruct((3, cells, rows, depth), jnp.float32),
             jax.ShapeDtypeStruct((cells, band, depth), jnp.float32),
         ),
-        in_specs=[on_vmem()] * 2,
+        in_specs=[on_vmem()],
         out_specs=(on_vmem(), on_vmem()),
         scratch_shapes=[
-            pltpu.VMEM((CORES * cells + 2 * HALO, tall, depth), jnp.float32),
+            pltpu.VMEM((wide, tall, depth), jnp.float32),
             pltpu.VMEM((3, cells + 2, tall, depth), jnp.float32),
             pltpu.VMEM((cells, fold_b * SUB, depth), jnp.float32),
             area(wide),
@@ -538,41 +527,40 @@
             window(wide - 2 + cells),
         ],
         compiler_params=pltpu.CompilerParams(vmem_limit_bytes=32 * 1024 * 1024),
-    )(chip, halo)
+    )(bands)
 
 
 def shards(density, void_depth, supports, load_x, load_y, load_vectors):
     cells, band, depth = density.shape
     groups = lax.axis_size("case")
-    slabs = lax.axis_size("column") * CORES
-    mine = packed(density, void_depth, supports, load_x, load_y, load_vectors)
-    chip = lax.all_to_all(mine, ("case", "core"), split_axis=0, concat_axis=0, tiled=True)
-    chip = chip.reshape(groups, CORES, cells + 1, band, depth)
-    low = chip[:, 0, :HALO]
-    high = chip[:, 1, cells - HALO : cells]
-    near = jnp.where(lax.axis_index("core") == 0, low, high)
-    pairs = [(i, i + 1) for i in range(1, slabs - 1, 2)]
-    pairs += [(j, i) for i, j in pairs]
-    halo = lax.ppermute(near, ("column", "core"), pairs)
-    field, sensitivity = relaxed(chip, halo)
+    slabs = lax.axis_size("space")
+    level = lax.broadcasted_iota(jnp.int32, density.shape, 2) - depth // 2
+    hollow = (level >= 0) & (level < void_depth[:, :, None])
+    solid = jnp.where(hollow, 0.0, density)
+    ahead = [(i, i + 1) for i in range(slabs - 1)]
+    behind = [(i + 1, i) for i in range(slabs - 1)]
+    low = lax.ppermute(solid[cells - HALO :], "space", ahead)
+    high = lax.ppermute(solid[:HALO], "space", behind)
+    row = settings(band, depth, supports, load_x, load_y, load_vectors)
+    mine = jnp.concatenate([low, solid, high, row])
+    mine = jnp.broadcast_to(mine[None], (groups, *mine.shape))
+    bands = lax.all_to_all(mine, "case", split_axis=0, concat_axis=0, tiled=True)
+    field, sensitivity = relaxed(bands)
     return (field[None], sensitivity)
 
 
 def solution(mesh):
-    groups, slabs = mesh.devices.shape
-    chips = Mesh(mesh.devices.reshape(groups, slabs // CORES, CORES), ("case", "column", "core"))
-    space = ("column", "core")
     return jax.shard_map(
         shards,
-        mesh=chips,
+        mesh=mesh,
         in_specs=(
-            P(space, "case", None),
-            P(space, "case"),
+            P("space", "case", None),
+            P("space", "case"),
             P("case", None),
             P("case"),
             P("case"),
             P("case", None, None),
         ),
-        out_specs=(P("case", None, space, None, None), P(space, "case", None)),
+        out_specs=(P("case", None, "space", None, None), P("space", "case", None)),
         check_vma=False,
     )

time: 28.6 us -> 27.5 us (0.962)
  the two profiles are of different devices: /device:TPU:1 before, /device:TPU:8 now
where the time goes in v2:
time: 27.5 us; the launch traced here: 27.2 us
  blocking collectives  9.64 us (35%)
  Pallas kernels  8.46 us (31%)
  starting transfers between devices  5.56 us (20%)
  between operations  1.98 us (7%)
  other arithmetic  1.52 us (6%)
    all_to_all x1, blocking collectives, shards(): lax.all_to_all(mine, 'case', split_axis=0, concat_axis=0, tiled=True)  9.64 us
    pallas_call x1, Pallas kernels, relaxed(): pl.pallas_call(relax_kernel, out_shape=(jax.ShapeDtypeStruct((3, cells, r...  7.08 us
    ppermute x1, starting transfers between devices, shards(): high = lax.ppermute(solid[:HALO], 'space', behind)  3.64 us
    ppermute x1, starting transfers between devices, shards(): low = lax.ppermute(solid[cells - HALO:], 'space', ahead)  1.92 us
    pallas_call x1, Pallas kernels, settings(): pl.pallas_call(settings_kernel, out_shape=jax.ShapeDtypeStruct((1, band,...  1.38 us
    select_n x1, other arithmetic, shards(): solid = jnp.where(hollow, 0.0, density)  0.82 us
    concatenate x1, other arithmetic, shards(): mine = jnp.concatenate([low, solid, high, row])  0.7 us
  transfers between devices with their start and end apart: 2, of which 0 were waited for; matrix products, arithmetic and copies ran while one was open for 0% of the time, Pallas kernels for 5%

profile of v2, /device:TPU:8, one launch (start us, length us, event | category | flops | bytes accessed | tf_op | source)
XLA Modules:
  0.0 27.2 jit_solution(2387679806652026056)
XLA Ops:
  0.7 0.8 %and_select_fusion = f32[6,8,128]{2,1,0:T(8,128)S(1)} fusion(f32[6,8,128]{2,1,0:T(8,128)} %param.6, s32[6,8]{1,0:T(8,128)} %param.7, s32[128]{0:T(128)S(1)} %iota_add_fusion, pred[128]{0:T(512)(128)(4,1)S(1)} %broadcast_compare_fusion), kind=kLoop, calls=%fused_computation.1 | loop fusion | flops 18432 | bytes 49984 | tf_op jit(solution)/shard_map/jit(_where)/select_n | solution.py:539
  1.5 1.9 %collective-permute-start = (f32[4,8,128]{2,1,0:T(8,128)S(1)}, f32[4,8,128]{2,1,0:T(8,128)S(1)}, u32[]{:S(2)}, u32[]{:S(2)}) collective-permute-start(f32[4,8,128]{2,1,0:T(8,128)S(1)} %get-tuple-element.6), channel_id=1, source_target_pairs={{0,1},{1,2},{2,3},{3,4},{4,5},{5,6},{6,7},{8,9},{9,10},{10,11},{11... | collective-permute-start | bytes 49160 | tf_op jit(solution)/shard_map/ppermute | solution.py:542
  3.4 3.6 %collective-permute-start.1 = (f32[4,8,128]{2,1,0:T(8,128)S(1)}, f32[4,8,128]{2,1,0:T(8,128)S(1)}, u32[]{:S(2)}, u32[]{:S(2)}) collective-permute-start(f32[4,8,128]{2,1,0:T(8,128)S(1)} %get-tuple-element.7), channel_id=1, source_target_pairs={{1,0},{2,1},{3,2},{4,3},{5,4},{6,5},{7,6},{9,8},{10,9},{11,10},{12... | collective-permute-start | bytes 49160 | tf_op jit(solution)/shard_map/ppermute | solution.py:543
  8.3 1.4 %shard_map.77 = f32[1,8,128]{2,1,0:T(8,128)} custom-call(s32[1,2]{1,0:T(1,128)} %supports_in.1, f32[3,1,48]{2,1,0:T(1,128)} %bitcast.2, s32[1]{0:T(128)S(6)} %copy.8.load_x_ref, s32[1]{0:T(128)S(6)} %copy.9.load_y_ref), custom_call_target="tpu_custom_call" | custom-call | tf_op jit(solution)/shard_map/pallas_call | solution.py:467
  9.7 0.0 collective-permute-done
  9.8 0.0 collective-permute-done.1
  9.8 0.7 %pad_maximum_fusion = f32[15,8,128]{2,1,0:T(8,128)S(1)} fusion(f32[1,8,128]{2,1,0:T(8,128)} %shard_map.77, f32[4,8,128]{2,1,0:T(8,128)S(1)} %collective-permute-done.1, f32[6,8,128]{2,1,0:T(8,128)S(1)} %and_select_fusion, f32[4,8,128]{2,1,0:T(8,128)S(1)} %collective-permute-done), kind=kLoop, calls=%fused_computation | loop fusion | flops 46080 | bytes 122880 | tf_op jit(solution)/shard_map/concatenate | solution.py:545
  10.5 9.6 %all_to_all.5.bands_ref = f32[4,15,8,128]{3,2,1,0:T(8,128)S(1)} all-to-all(f32[4,15,8,128]{3,2,1,0:T(8,128)S(1)} %broadcast_in_dim.15), channel_id=1, replica_groups=mesh['case'=4,'space'=8] {'case'}, dimensions={0} | all-to-all | bytes 491520 | tf_op jit(solution)/shard_map/all_to_all | solution.py:547
  20.1 7.1 %shard_map.78 = (f32[3,6,32,128]{3,2,1,0:T(8,128)}, f32[6,8,128]{2,1,0:T(8,128)}) custom-call(f32[4,15,8,128]{3,2,1,0:T(8,128)S(1)} %all_to_all.5.bands_ref), custom_call_target="tpu_custom_call" | custom-call | tf_op jit(solution)/shard_map/pallas_call | solution.py:499
  (4 shorter events, 0.0 us)
Async XLA Ops:
  1.5 8.3 %collective-permute-start = (f32[4,8,128]{2,1,0:T(8,128)S(1)}, f32[4,8,128]{2,1,0:T(8,128)S(1)}, u32[]{:S(2)}, u32[]{:S(2)}) collective-permute-start(f32[4,8,128]{2,1,0:T(8,128)S(1)} %get-tuple-element.6), channel_id=1, source_target_pairs={{0,1},{1,2},{2,3},{3,4},{4,5},{5,6},{6,7},{8,9},{9,10},{10,11},{11... | collective-permute-start | bytes 49160 | tf_op jit(solution)/shard_map/ppermute | solution.py:542
  3.4 6.3 %collective-permute-start.1 = (f32[4,8,128]{2,1,0:T(8,128)S(1)}, f32[4,8,128]{2,1,0:T(8,128)S(1)}, u32[]{:S(2)}, u32[]{:S(2)}) collective-permute-start(f32[4,8,128]{2,1,0:T(8,128)S(1)} %get-tuple-element.7), channel_id=1, source_target_pairs={{1,0},{2,1},{3,2},{4,3},{5,4},{6,5},{7,6},{9,8},{10,9},{11,10},{12... | collective-permute-start | bytes 49160 | tf_op jit(solution)/shard_map/ppermute | solution.py:543

commit v3 on v2

--- a/solution.py
+++ b/solution.py
@@ -14,6 +14,7 @@
 UPPER = 3.0
 PATCH = 4.0
 SUB = 8
+CORES = 2
 HALO = SWEEPS + 1
 EDGE = HALO - 1
 PAD = 8
@@ -466,7 +467,7 @@
     vectors = load_vectors.transpose(1, 0, 2)
     return pl.pallas_call(
         settings_kernel,
-        out_shape=jax.ShapeDtypeStruct((1, band, depth), jnp.float32),
+        out_shape=pltpu.VMEM((1, band, depth), jnp.float32),
         in_specs=[pl.BlockSpec(memory_space=pltpu.HBM)] * 2 + [on_smem()] * 2,
         out_specs=on_vmem(),
         scratch_shapes=[
@@ -537,12 +538,19 @@
     level = lax.broadcasted_iota(jnp.int32, density.shape, 2) - depth // 2
     hollow = (level >= 0) & (level < void_depth[:, :, None])
     solid = jnp.where(hollow, 0.0, density)
-    ahead = [(i, i + 1) for i in range(slabs - 1)]
-    behind = [(i + 1, i) for i in range(slabs - 1)]
-    low = lax.ppermute(solid[cells - HALO :], "space", ahead)
-    high = lax.ppermute(solid[:HALO], "space", behind)
+    across = [(i, i + 1) for i in range(1, slabs - 1, 2)]
+    across += [(j, i) for i, j in across]
+    inside = [(i, i + 1) for i in range(0, slabs, 2)]
+    inside += [(j, i) for i, j in inside]
+    first = lax.rem(lax.axis_index("space"), CORES) == 0
+    low = solid[:HALO]
+    high = solid[cells - HALO :]
+    outer = lax.ppermute(jnp.where(first, low, high), "space", across)
+    inner = lax.ppermute(jnp.where(first, high, low), "space", inside)
     row = settings(band, depth, supports, load_x, load_y, load_vectors)
-    mine = jnp.concatenate([low, solid, high, row])
+    before = jnp.where(first, outer, inner)
+    after = jnp.where(first, inner, outer)
+    mine = jnp.concatenate([before, solid, after, row])
     mine = jnp.broadcast_to(mine[None], (groups, *mine.shape))
     bands = lax.all_to_all(mine, "case", split_axis=0, concat_axis=0, tiled=True)
     field, sensitivity = relaxed(bands)

time: 27.5 us -> 26.1 us (0.949)
  the two profiles are of different devices: /device:TPU:8 before, /device:TPU:0 now
where the time goes in v3:
time: 26.1 us; the launch traced here: 25.8 us
  blocking collectives  9.27 us (36%)
  Pallas kernels  7.87 us (30%)
  starting transfers between devices  5.11 us (20%)
  between operations  2.02 us (8%)
  other arithmetic  0.84 us (3%)
  local copies, waits for them, and re-layouts  0.7 us (3%)
    all_to_all x1, blocking collectives, shards(): lax.all_to_all(mine, 'case', split_axis=0, concat_axis=0, tiled=True)  9.27 us
    pallas_call x1, Pallas kernels, relaxed(): pl.pallas_call(relax_kernel, out_shape=(jax.ShapeDtypeStruct((3, cells, r...  7.08 us
    ppermute x1, starting transfers between devices, shards(): inner = lax.ppermute(jnp.where(first, high, low), 'space', inside)  4.45 us
    select_n x1, other arithmetic, shards(): solid = jnp.where(hollow, 0.0, density)  0.81 us
    pallas_call x1, Pallas kernels, settings(): pl.pallas_call(settings_kernel, out_shape=pltpu.VMEM((1, band, depth), jn...  0.79 us
    unnamed x2, local copies, waits for them, and re-layouts  0.68 us
    ppermute x1, starting transfers between devices, shards(): outer = lax.ppermute(jnp.where(first, low, high), 'space', across)  0.66 us
  transfers between devices with their start and end apart: 2, of which 0 were waited for; matrix products, arithmetic and copies ran while one was open for 0% of the time, Pallas kernels for 3%

profile of v3, /device:TPU:0, one launch (start us, length us, event | category | flops | bytes accessed | tf_op | source)
XLA Modules:
  0.0 25.8 jit_solution(4209104683004159633)
XLA Ops:
  0.7 0.0 copy-start
  0.7 0.7 %copy-done = s32[6,8]{1,0:T(8,128)S(1)} copy-done((s32[6,8]{1,0:T(8,128)S(1)}, s32[6,8]{1,0:T(8,128)}, u32[]{:S(2)}) %copy-start) | copy-done | bytes 216
  1.3 0.8 %and_select_fusion = f32[6,8,128]{2,1,0:T(8,128)S(1)} fusion(f32[6,8,128]{2,1,0:T(8,128)} %param.6, s32[6,8]{1,0:T(8,128)S(1)} %copy-done, s32[128]{0:T(128)S(1)} %iota_add_fusion, pred[128]{0:T(512)(128)(4,1)S(1)} %broadcast_compare_fusion), kind=kLoop, calls=%fused_computation.1 | loop fusion | flops 18432 | bytes 49984 | tf_op jit(solution)/shard_map/jit(_where)/select_n | solution.py:540
  2.2 0.7 %collective-permute-start = (f32[4,8,128]{2,1,0:T(8,128)S(1)}, f32[4,8,128]{2,1,0:T(8,128)S(1)}, u32[]{:S(2)}, u32[]{:S(2)}) collective-permute-start(f32[4,8,128]{2,1,0:T(8,128)S(1)} %get-tuple-element.8), channel_id=1, source_target_pairs={{1,2},{3,4},{5,6},{2,1},{4,3},{6,5},{9,10},{11,12},{13,14},{10,9},... | collective-permute-start | bytes 49160 | tf_op jit(solution)/shard_map/ppermute | solution.py:548
  2.8 4.5 %collective-permute-start.1 = (f32[4,8,128]{2,1,0:T(8,128)S(1)}, f32[4,8,128]{2,1,0:T(8,128)S(1)}, u32[]{:S(2)}, u32[]{:S(2)}) collective-permute-start(f32[4,8,128]{2,1,0:T(8,128)S(1)} %get-tuple-element.9), channel_id=1, source_target_pairs={{0,1},{2,3},{4,5},{6,7},{1,0},{3,2},{5,4},{7,6},{8,9},{10,11},{12,... | collective-permute-start | bytes 49160 | tf_op jit(solution)/shard_map/ppermute | solution.py:549
  8.6 0.8 %shard_map.77 = f32[1,8,128]{2,1,0:T(8,128)S(1)} custom-call(s32[1,2]{1,0:T(1,128)} %supports_in.1, f32[3,1,48]{2,1,0:T(1,128)} %bitcast.2, s32[1]{0:T(128)S(6)} %copy.8.load_x_ref, s32[1]{0:T(128)S(6)} %copy.9.load_y_ref), custom_call_target="tpu_custom_call" | custom-call | tf_op jit(solution)/shard_map/pallas_call | solution.py:468
  9.4 0.0 collective-permute-done
  9.4 0.0 collective-permute-done.1
  9.5 9.3 %all_to_all.5.bands_ref = f32[4,15,8,128]{3,2,1,0:T(8,128)S(1)} all-to-all(f32[4,15,8,128]{3,2,1,0:T(8,128)S(1)} %broadcast_in_dim.15), channel_id=1, replica_groups=mesh['case'=4,'space'=8] {'case'}, dimensions={0} | all-to-all | bytes 491520 | tf_op jit(solution)/shard_map/all_to_all | solution.py:555
  18.7 7.1 %shard_map.78 = (f32[3,6,32,128]{3,2,1,0:T(8,128)}, f32[6,8,128]{2,1,0:T(8,128)}) custom-call(f32[4,15,8,128]{3,2,1,0:T(8,128)S(1)} %all_to_all.5.bands_ref), custom_call_target="tpu_custom_call" | custom-call | tf_op jit(solution)/shard_map/pallas_call | solution.py:500
  (6 shorter events, 0.1 us)
Async XLA Ops:
  0.7 0.7 %copy-start = (s32[6,8]{1,0:T(8,128)S(1)}, s32[6,8]{1,0:T(8,128)}, u32[]{:S(2)}) copy-start(s32[6,8]{1,0:T(8,128)} %param.7) | copy-start | bytes 580
  2.2 7.2 %collective-permute-start = (f32[4,8,128]{2,1,0:T(8,128)S(1)}, f32[4,8,128]{2,1,0:T(8,128)S(1)}, u32[]{:S(2)}, u32[]{:S(2)}) collective-permute-start(f32[4,8,128]{2,1,0:T(8,128)S(1)} %get-tuple-element.8), channel_id=1, source_target_pairs={{1,2},{3,4},{5,6},{2,1},{4,3},{6,5},{9,10},{11,12},{13,14},{10,9},... | collective-permute-start | bytes 49160 | tf_op jit(solution)/shard_map/ppermute | solution.py:548
  2.8 6.6 %collective-permute-start.1 = (f32[4,8,128]{2,1,0:T(8,128)S(1)}, f32[4,8,128]{2,1,0:T(8,128)S(1)}, u32[]{:S(2)}, u32[]{:S(2)}) collective-permute-start(f32[4,8,128]{2,1,0:T(8,128)S(1)} %get-tuple-element.9), channel_id=1, source_target_pairs={{0,1},{2,3},{4,5},{6,7},{1,0},{3,2},{5,4},{7,6},{8,9},{10,11},{12,... | collective-permute-start | bytes 49160 | tf_op jit(solution)/shard_map/ppermute | solution.py:549

commit v4 on v3

--- a/solution.py
+++ b/solution.py
@@ -50,6 +50,36 @@
 
 def span_of(cells):
     return cells + 2 * EDGE
+
+
+def solid_kernel(
+    density_in, void_in, solid_ref, outer_ref, inner_ref, density_ref, void_ref, arrived
+):
+    fetches = [
+        pltpu.make_async_copy(void_in, void_ref, arrived.at[0]),
+        pltpu.make_async_copy(density_in, density_ref, arrived.at[1]),
+    ]
+    for fetch in fetches:
+        fetch.start()
+    cells, band, depth = solid_ref.shape
+    first = lax.rem(lax.axis_index("space"), CORES) == 0
+    level = lax.broadcasted_iota(jnp.int32, (band, depth), 1) - depth // 2
+    eye = lax.broadcasted_iota(jnp.int32, (band, band), 0) == lax.broadcasted_iota(
+        jnp.int32, (band, band), 1
+    )
+    for fetch in fetches:
+        fetch.wait()
+    for i in range(cells):
+        line = jnp.broadcast_to(void_ref[i : i + 1, :], (band, band)).astype(jnp.float32)
+        column = jnp.sum(jnp.where(eye, line, 0.0), axis=1, keepdims=True)
+        top = jnp.broadcast_to(column, (band, depth)).astype(jnp.int32)
+        hollow = (level >= 0) & (level < top)
+        solid_ref[i] = jnp.where(hollow, 0.0, density_ref[i])
+    for i in range(HALO):
+        low = solid_ref[i]
+        high = solid_ref[cells - HALO + i]
+        outer_ref[i] = jnp.where(first, low, high)
+        inner_ref[i] = jnp.where(first, high, low)
 
 
 def settings_kernel(
@@ -463,6 +493,23 @@
     return pl.BlockSpec(memory_space=pltpu.SMEM)
 
 
+def solids(density, void_depth):
+    cells, band, depth = density.shape
+    return pl.pallas_call(
+        solid_kernel,
+        out_shape=[
+            pltpu.VMEM((planes, band, depth), jnp.float32) for planes in (cells, HALO, HALO)
+        ],
+        in_specs=[pl.BlockSpec(memory_space=pltpu.HBM)] * 2,
+        out_specs=[on_vmem()] * 3,
+        scratch_shapes=[
+            pltpu.VMEM(density.shape, jnp.float32),
+            pltpu.VMEM(void_depth.shape, jnp.int32),
+            pltpu.SemaphoreType.DMA((2,)),
+        ],
+    )(*(pltpu.with_memory_space_constraint(array, pltpu.HBM) for array in (density, void_depth)))
+
+
 def settings(band, depth, supports, load_x, load_y, load_vectors):
     vectors = load_vectors.transpose(1, 0, 2)
     return pl.pallas_call(
@@ -535,18 +582,14 @@
     cells, band, depth = density.shape
     groups = lax.axis_size("case")
     slabs = lax.axis_size("space")
-    level = lax.broadcasted_iota(jnp.int32, density.shape, 2) - depth // 2
-    hollow = (level >= 0) & (level < void_depth[:, :, None])
-    solid = jnp.where(hollow, 0.0, density)
+    solid, far, near = solids(density, void_depth)
     across = [(i, i + 1) for i in range(1, slabs - 1, 2)]
     across += [(j, i) for i, j in across]
     inside = [(i, i + 1) for i in range(0, slabs, 2)]
     inside += [(j, i) for i, j in inside]
     first = lax.rem(lax.axis_index("space"), CORES) == 0
-    low = solid[:HALO]
-    high = solid[cells - HALO :]
-    outer = lax.ppermute(jnp.where(first, low, high), "space", across)
-    inner = lax.ppermute(jnp.where(first, high, low), "space", inside)
+    outer = lax.ppermute(far, "space", across)
+    inner = lax.ppermute(near, "space", inside)
     row = settings(band, depth, supports, load_x, load_y, load_vectors)
     before = jnp.where(first, outer, inner)
     after = jnp.where(first, inner, outer)

time: 26.1 us -> 25.4 us (0.973)
  Pallas kernels: 7.87 us -> 8.73 us
  other arithmetic: 0.84 us -> 0.02 us
  local copies, waits for them, and re-layouts: 0.7 us -> 0.02 us
    pallas_call x0 -> x1, Pallas kernels: none -> 0.86 us  [solids(): pl.pallas_call(solid_kernel, out_shape=[pltpu.VMEM((planes, band, depth),...]
    select_n x2 -> x0, other arithmetic: 0.82 us -> none  [the longest x1 0.81 us: shards(): solid = jnp.where(hollow, 0.0, density)]
    unnamed x2 -> x0, local copies, waits for them, and re-layouts: 0.68 us -> none
where the time goes in v4:
time: 25.4 us; the launch traced here: 25.2 us
  blocking collectives  9.28 us (37%)
  Pallas kernels  8.73 us (34%)
  starting transfers between devices  5.11 us (20%)
  between operations  1.99 us (8%)
    all_to_all x1, blocking collectives, shards(): lax.all_to_all(mine, 'case', split_axis=0, concat_axis=0, tiled=True)  9.28 us
    pallas_call x1, Pallas kernels, relaxed(): pl.pallas_call(relax_kernel, out_shape=(jax.ShapeDtypeStruct((3, cells, r...  7.08 us
    ppermute x1, starting transfers between devices, shards(): inner = lax.ppermute(near, 'space', inside)  4.45 us
    pallas_call x1, Pallas kernels, solids(): pl.pallas_call(solid_kernel, out_shape=[pltpu.VMEM((planes, band, depth),...  0.86 us
    pallas_call x1, Pallas kernels, settings(): pl.pallas_call(settings_kernel, out_shape=pltpu.VMEM((1, band, depth), jn...  0.79 us
    ppermute x1, starting transfers between devices, shards(): outer = lax.ppermute(far, 'space', across)  0.66 us
  transfers between devices with their start and end apart: 2, of which 0 were waited for; matrix products, arithmetic and copies ran while one was open for 0% of the time, Pallas kernels for 3%

profile of v4, /device:TPU:0, one launch (start us, length us, event | category | flops | bytes accessed | tf_op | source)
XLA Modules:
  0.0 25.2 jit_solution(3396242557670454159)
XLA Ops:
  0.6 0.9 %shard_map.77 = (f32[6,8,128]{2,1,0:T(8,128)S(1)}, f32[4,8,128]{2,1,0:T(8,128)S(1)}, f32[4,8,128]{2,1,0:T(8,128)S(1)}) custom-call(f32[6,8,128]{2,1,0:T(8,128)} %density_in.1, s32[6,8]{1,0:T(8,128)} %void_in.1), custom_call_target="tpu_custom_call" | custom-call | tf_op jit(solution)/shard_map/pallas_call | solution.py:498
  1.5 0.7 %collective-permute-start = (f32[4,8,128]{2,1,0:T(8,128)S(1)}, f32[4,8,128]{2,1,0:T(8,128)S(1)}, u32[]{:S(2)}, u32[]{:S(2)}) collective-permute-start(f32[4,8,128]{2,1,0:T(8,128)S(1)} %get-tuple-element.7), channel_id=1, source_target_pairs={{1,2},{3,4},{5,6},{2,1},{4,3},{6,5},{9,10},{11,12},{13,14},{10,9},... | collective-permute-start | bytes 49160 | tf_op jit(solution)/shard_map/ppermute | solution.py:591
  2.2 4.5 %collective-permute-start.1 = (f32[4,8,128]{2,1,0:T(8,128)S(1)}, f32[4,8,128]{2,1,0:T(8,128)S(1)}, u32[]{:S(2)}, u32[]{:S(2)}) collective-permute-start(f32[4,8,128]{2,1,0:T(8,128)S(1)} %get-tuple-element.8), channel_id=1, source_target_pairs={{0,1},{2,3},{4,5},{6,7},{1,0},{3,2},{5,4},{7,6},{8,9},{10,11},{12,... | collective-permute-start | bytes 49160 | tf_op jit(solution)/shard_map/ppermute | solution.py:592
  7.9 0.8 %shard_map.78 = f32[1,8,128]{2,1,0:T(8,128)S(1)} custom-call(s32[1,2]{1,0:T(1,128)} %supports_in.1, f32[3,1,48]{2,1,0:T(1,128)} %bitcast.2, s32[1]{0:T(128)S(6)} %copy.8.load_x_ref, s32[1]{0:T(128)S(6)} %copy.9.load_y_ref), custom_call_target="tpu_custom_call" | custom-call | tf_op jit(solution)/shard_map/pallas_call | solution.py:515
  8.7 0.0 collective-permute-done
  8.7 0.0 collective-permute-done.1
  8.8 9.3 %all_to_all.5.bands_ref = f32[4,15,8,128]{3,2,1,0:T(8,128)S(1)} all-to-all(f32[4,15,8,128]{3,2,1,0:T(8,128)S(1)} %broadcast_in_dim.4), channel_id=1, replica_groups=mesh['case'=4,'space'=8] {'case'}, dimensions={0} | all-to-all | bytes 491520 | tf_op jit(solution)/shard_map/all_to_all | solution.py:598
  18.1 7.1 %shard_map.79 = (f32[3,6,32,128]{3,2,1,0:T(8,128)}, f32[6,8,128]{2,1,0:T(8,128)}) custom-call(f32[4,15,8,128]{3,2,1,0:T(8,128)S(1)} %all_to_all.5.bands_ref), custom_call_target="tpu_custom_call" | custom-call | tf_op jit(solution)/shard_map/pallas_call | solution.py:547
  (3 shorter events, 0.0 us)
Async XLA Ops:
  1.5 7.2 %collective-permute-start = (f32[4,8,128]{2,1,0:T(8,128)S(1)}, f32[4,8,128]{2,1,0:T(8,128)S(1)}, u32[]{:S(2)}, u32[]{:S(2)}) collective-permute-start(f32[4,8,128]{2,1,0:T(8,128)S(1)} %get-tuple-element.7), channel_id=1, source_target_pairs={{1,2},{3,4},{5,6},{2,1},{4,3},{6,5},{9,10},{11,12},{13,14},{10,9},... | collective-permute-start | bytes 49160 | tf_op jit(solution)/shard_map/ppermute | solution.py:591
  2.2 6.6 %collective-permute-start.1 = (f32[4,8,128]{2,1,0:T(8,128)S(1)}, f32[4,8,128]{2,1,0:T(8,128)S(1)}, u32[]{:S(2)}, u32[]{:S(2)}) collective-permute-start(f32[4,8,128]{2,1,0:T(8,128)S(1)} %get-tuple-element.8), channel_id=1, source_target_pairs={{0,1},{2,3},{4,5},{6,7},{1,0},{3,2},{5,4},{7,6},{8,9},{10,11},{12,... | collective-permute-start | bytes 49160 | tf_op jit(solution)/shard_map/ppermute | solution.py:592

commit v5 on v4

--- a/solution.py
+++ b/solution.py
@@ -141,6 +141,8 @@
     second_b,
     squares_b,
     work_b,
+    field_v,
+    gone,
 ):
     groups, planes, band, depth = bands_ref.shape
     wide = planes - 1
@@ -151,6 +153,7 @@
     total_x = lax.axis_size("space") * cells
     first_plane = lax.axis_index("space") * cells
     omegas = relaxations(SWEEPS)
+    scale = omegas[0] * omegas[1] * omegas[2]
 
     blank = jnp.zeros((PAD, depth), jnp.float32)
     for i in range(wide):
@@ -173,6 +176,8 @@
     not_first_s = (line > 0).astype(jnp.float32)
     not_last_s = (line < SUB - 1).astype(jnp.float32)
     at_bottom = (lane == 0).astype(jnp.float32)
+    half_first_z = 0.5 * not_first_z
+    half_last_z = 0.5 * not_last_z
 
     def along_z(a):
         after = pltpu.roll(a, depth - 1, 2) * not_last_z
@@ -230,7 +235,7 @@
                 inv_s[i - 1] = inv_root
             if factor_s is not None and HALO <= i < HALO + cells:
                 ratio = solid * inv_root
-                factor_s[i - HALO] = ((-1.5 * (1.0 - EMIN)) / groups) * (ratio * ratio)
+                factor_s[i - HALO] = ((-1.5 * (1.0 - EMIN)) * scale * scale / groups) * (ratio * ratio)
 
     def tensor_parts(r, closed):
         zs, zd = both(along_z(r))
@@ -286,48 +291,53 @@
         return value
 
     def field_parts(w, closed):
-        pair = [both(along_z(w[k])) for k in range(3)]
-        zs = [pair[k][0] for k in range(3)]
-        zd = [pair[k][1] for k in range(3)]
-        ysx, ydx = both(along_y(w[0], closed))
-        ysy, ydy = both(along_y(w[1], closed))
-        ysz = plus(along_y(w[2], closed))
-        yszsx, ydzsx = both(along_y(zs[0], closed))
-        yszsy, ydzsy = both(along_y(zs[1], closed))
-        yszsz = plus(along_y(zs[2], closed))
-        yszdx = plus(along_y(zd[0], closed))
-        ydzdy = minus(along_y(zd[1], closed))
-        yszdz, ydzdz = both(along_y(zd[2], closed))
+        zs, zd = [], []
+        for k in range(3):
+            after = pltpu.roll(w[k], depth - 1, 2) * half_last_z
+            before = pltpu.roll(w[k], 1, 2) * half_first_z
+            zs.append(after + before)
+            zd.append(after - before)
+        mean = [w[k] + zs[k] for k in range(2)]
+        mixed = [CROSS2 * w[k] + (2.0 * CROSS3) * zs[k] for k in range(2)]
+        even_y = [plus(along_y(0.5 * mean[k] + mixed[k], closed)) for k in range(2)]
+        odd_y = [minus(along_y(mixed[k], closed)) for k in range(2)]
+        strong = [(2.0 * PAIR) * mean[k] + (AXIAL - 2.0 * PAIR) * w[k] for k in range(2)]
+        upright = w[2] + (2.0 * PAIR) * zs[2]
+        flat = FLAT * w[2] + (2.0 * FULL) * zs[2]
+        twist_y = minus(along_y(zd[1], closed))
+        spread_z, twist_z = both(along_y(zd[2], closed))
+        slope_x = (2.0 * CROSS2) * zd[0] + (2.0 * CROSS3) * plus(along_y(zd[0], closed))
+        slope_z = (2.0 * CROSS2) * zd[2] + (2.0 * CROSS3) * spread_z
         here = [
-            ysx + FLAT * yszsx + zs[0],
-            AXIAL * ysy + PAIR * yszsy + zs[1] + CROSS2 * ydzdz,
-            ysz + PAIR * yszsz + AXIAL * zs[2] + CROSS2 * ydzdy,
+            plus(along_y(mean[0], closed)) + (zs[0] + zs[0]),
+            plus(along_y(strong[1], closed)) + (zs[1] + zs[1]) + (2.0 * CROSS2) * twist_z,
+            plus(along_y(upright, closed)) + (2.0 * AXIAL) * zs[2] + (2.0 * CROSS2) * twist_y,
         ]
         even = [
-            AXIAL * w[0] + PAIR * (zs[0] + ysx) + FULL * yszsx,
-            w[1] + FLAT * zs[1] + PAIR * ysy + FULL * yszsy + CROSS3 * ydzdz,
-            w[2] + PAIR * zs[2] + FLAT * ysz + FULL * yszsz + CROSS3 * ydzdy,
+            strong[0] + even_y[0],
+            mean[1] + even_y[1] + (2.0 * CROSS3) * twist_z,
+            upright + plus(along_y(flat, closed)) + (2.0 * CROSS3) * twist_y,
         ]
-        odd = [
-            CROSS2 * (ydy + zd[2]) + CROSS3 * (ydzsy + yszdz),
-            CROSS2 * ydx + CROSS3 * ydzsx,
-            CROSS2 * zd[0] + CROSS3 * yszdx,
-        ]
+        odd = [odd_y[1] + slope_z, odd_y[0], slope_x]
         ahead = [even[k] + odd[k] for k in range(3)]
         behind = [even[k] - odd[k] for k in range(3)]
         return here, ahead, behind
 
-    def sweep(closed, count, load, omega, value, store, root_s, push_s, inverse_s, shear_s):
+    def sweep(closed, count, load, keep, drive, value, store, root_s, push_s, inverse_s, shear_s):
         offset = (wide - count) // 2
         partial = None
         trail = None
+        free = None
         for i in range(count):
+            held = free
             r = root_s[i + offset]
+            if drive is not None:
+                free = 1.0 - value(3, i + offset - 1) * at_bottom
+                r = r * free
             here, ahead, behind = field_parts([r * load(k, i) for k in range(3)], closed)
             if i >= 2:
                 j = i - 1
                 d = j + offset - 1
-                free = 1.0 - value(3, d) * at_bottom
                 old = [load(k, j) for k in range(3)]
                 shear = [shear_s[k, d] for k in range(3)]
                 rest = [
@@ -336,11 +346,17 @@
                     shear[1] * old[0] + shear[2] * old[1],
                 ]
                 for k in range(3):
-                    pull = (partial[k] + ahead[k] - rest[k]) * (inverse_s[k, d] * free)
-                    store(k, j - 1, (1.0 - omega) * old[k] + omega * (push_s[k, d] + pull))
+                    new = keep * old[k] + (partial[k] + ahead[k] - rest[k]) * inverse_s[k, d]
+                    if drive is not None:
+                        new = (new + drive * push_s[k, d]) * held
+                    store(k, j - 1, new)
             if i >= 1:
                 partial = [here[k] + trail[k] for k in range(3)]
             trail = behind
+
+    keep_second = (1.0 - omegas[1]) / omegas[1] + 1.0 / omegas[0]
+    keep_third = (1.0 - omegas[2]) / omegas[2]
+    drive_third = 1.0 / (omegas[0] * omegas[1])
 
     fold = rows // SUB
     inv_a = first_a.at[0]
@@ -355,13 +371,24 @@
         for t in range(fold):
             third_n[k, i, pl.ds(PAD + t, SUB, stride=fold), :] = new[t]
             if 1 <= i <= cells:
-                field_ref[k, i - 1, pl.ds(t, SUB, stride=fold), :] = new[t]
+                field_v[k, i - 1, pl.ds(t, SUB, stride=fold), :] = scale * new[t]
 
     arrays = (root_a, push_a, inverse_a, shear_a)
     sweep(
-        True, wide - 2, lambda k, i: omegas[0] * push_a[k, i], omegas[1], value, store_first_a, *arrays
+        True, wide - 2, lambda k, i: push_a[k, i], keep_second, None, value, store_first_a, *arrays
     )
-    sweep(True, wide - 4, lambda k, i: first_a[k, i], omegas[2], value, store_third_a, *arrays)
+    sweep(
+        True,
+        wide - 4,
+        lambda k, i: first_a[k, i],
+        keep_third,
+        drive_third,
+        value,
+        store_third_a,
+        *arrays,
+    )
+    leaving = pltpu.make_async_copy(field_v, field_ref, gone.at[0])
+    leaving.start()
 
     fold_b = result_n.shape[1] // SUB
     top = case * band - HALO
@@ -405,14 +432,22 @@
             sweep(
                 False,
                 wide - 2,
-                lambda k, i: omegas[0] * push_b[k, i],
-                omegas[1],
+                lambda k, i: push_b[k, i],
+                keep_second,
+                None,
                 value,
                 store_first_b,
                 *arrays,
             )
             sweep(
-                False, wide - 4, lambda k, i: first_b[k, i], omegas[2], value, store_second_b, *arrays
+                False,
+                wide - 4,
+                lambda k, i: first_b[k, i],
+                keep_third,
+                drive_third,
+                value,
+                store_second_b,
+                *arrays,
             )
 
         partial = None
@@ -483,6 +518,7 @@
             partial = here + trail
         trail = behind
     sensitivity_ref[...] = result_n[:, HALO : HALO + band, :]
+    leaving.wait()
 
 
 def on_vmem():
@@ -551,7 +587,7 @@
             jax.ShapeDtypeStruct((cells, band, depth), jnp.float32),
         ),
         in_specs=[on_vmem()],
-        out_specs=(on_vmem(), on_vmem()),
+        out_specs=(pl.BlockSpec(memory_space=pltpu.HBM), on_vmem()),
         scratch_shapes=[
             pltpu.VMEM((wide, tall, depth), jnp.float32),
             pltpu.VMEM((3, cells + 2, tall, depth), jnp.float32),
@@ -573,6 +609,8 @@
             window(3, cells + 2),
             window(6, cells + 2),
             window(wide - 2 + cells),
+            pltpu.VMEM((3, cells, rows, depth), jnp.float32),
+            pltpu.SemaphoreType.DMA((1,)),
         ],
         compiler_params=pltpu.CompilerParams(vmem_limit_bytes=32 * 1024 * 1024),
     )(bands)

time: 25.4 us -> 25.4 us (level)
  no operation moved by 1% of the time
where the time goes in v5:
time: 25.4 us; the launch traced here: 25.1 us
  blocking collectives  9.28 us (37%)
  Pallas kernels  8.71 us (34%)
  starting transfers between devices  5.11 us (20%)
  between operations  1.99 us (8%)
    all_to_all x1, blocking collectives, shards(): lax.all_to_all(mine, 'case', split_axis=0, concat_axis=0, tiled=True)  9.28 us
    pallas_call x1, Pallas kernels, relaxed(): pl.pallas_call(relax_kernel, out_shape=(jax.ShapeDtypeStruct((3, cells, r...  7.06 us
    ppermute x1, starting transfers between devices, shards(): inner = lax.ppermute(near, 'space', inside)  4.45 us
    pallas_call x1, Pallas kernels, solids(): pl.pallas_call(solid_kernel, out_shape=[pltpu.VMEM((planes, band, depth),...  0.86 us
    pallas_call x1, Pallas kernels, settings(): pl.pallas_call(settings_kernel, out_shape=pltpu.VMEM((1, band, depth), jn...  0.79 us
    ppermute x1, starting transfers between devices, shards(): outer = lax.ppermute(far, 'space', across)  0.66 us
  transfers between devices with their start and end apart: 2, of which 0 were waited for; matrix products, arithmetic and copies ran while one was open for 0% of the time, Pallas kernels for 3%

profile of v5, /device:TPU:0, one launch (start us, length us, event | category | flops | bytes accessed | tf_op | source)
XLA Modules:
  0.0 25.1 jit_solution(6497999671034458758)
XLA Ops:
  0.6 0.9 %shard_map.77 = (f32[6,8,128]{2,1,0:T(8,128)S(1)}, f32[4,8,128]{2,1,0:T(8,128)S(1)}, f32[4,8,128]{2,1,0:T(8,128)S(1)}) custom-call(f32[6,8,128]{2,1,0:T(8,128)} %density_in.1, s32[6,8]{1,0:T(8,128)} %void_in.1), custom_call_target="tpu_custom_call" | custom-call | tf_op jit(solution)/shard_map/pallas_call | solution.py:534
  1.5 0.7 %collective-permute-start = (f32[4,8,128]{2,1,0:T(8,128)S(1)}, f32[4,8,128]{2,1,0:T(8,128)S(1)}, u32[]{:S(2)}, u32[]{:S(2)}) collective-permute-start(f32[4,8,128]{2,1,0:T(8,128)S(1)} %get-tuple-element.7), channel_id=1, source_target_pairs={{1,2},{3,4},{5,6},{2,1},{4,3},{6,5},{9,10},{11,12},{13,14},{10,9},... | collective-permute-start | bytes 49160 | tf_op jit(solution)/shard_map/ppermute | solution.py:629
  2.2 4.5 %collective-permute-start.1 = (f32[4,8,128]{2,1,0:T(8,128)S(1)}, f32[4,8,128]{2,1,0:T(8,128)S(1)}, u32[]{:S(2)}, u32[]{:S(2)}) collective-permute-start(f32[4,8,128]{2,1,0:T(8,128)S(1)} %get-tuple-element.8), channel_id=1, source_target_pairs={{0,1},{2,3},{4,5},{6,7},{1,0},{3,2},{5,4},{7,6},{8,9},{10,11},{12,... | collective-permute-start | bytes 49160 | tf_op jit(solution)/shard_map/ppermute | solution.py:630
  7.9 0.8 %shard_map.78 = f32[1,8,128]{2,1,0:T(8,128)S(1)} custom-call(s32[1,2]{1,0:T(1,128)} %supports_in.1, f32[3,1,48]{2,1,0:T(1,128)} %bitcast.2, s32[1]{0:T(128)S(6)} %copy.8.load_x_ref, s32[1]{0:T(128)S(6)} %copy.9.load_y_ref), custom_call_target="tpu_custom_call" | custom-call | tf_op jit(solution)/shard_map/pallas_call | solution.py:551
  8.7 0.0 collective-permute-done
  8.7 0.0 collective-permute-done.1
  8.8 9.3 %all_to_all.5.bands_ref = f32[4,15,8,128]{3,2,1,0:T(8,128)S(1)} all-to-all(f32[4,15,8,128]{3,2,1,0:T(8,128)S(1)} %broadcast_in_dim.4), channel_id=1, replica_groups=mesh['case'=4,'space'=8] {'case'}, dimensions={0} | all-to-all | bytes 491520 | tf_op jit(solution)/shard_map/all_to_all | solution.py:636
  18.1 7.1 %shard_map.79 = (f32[3,6,32,128]{3,2,1,0:T(8,128)}, f32[6,8,128]{2,1,0:T(8,128)}) custom-call(f32[4,15,8,128]{3,2,1,0:T(8,128)S(1)} %all_to_all.5.bands_ref), custom_call_target="tpu_custom_call" | custom-call | tf_op jit(solution)/shard_map/pallas_call | solution.py:583
  (3 shorter events, 0.0 us)
Async XLA Ops:
  1.5 7.2 %collective-permute-start = (f32[4,8,128]{2,1,0:T(8,128)S(1)}, f32[4,8,128]{2,1,0:T(8,128)S(1)}, u32[]{:S(2)}, u32[]{:S(2)}) collective-permute-start(f32[4,8,128]{2,1,0:T(8,128)S(1)} %get-tuple-element.7), channel_id=1, source_target_pairs={{1,2},{3,4},{5,6},{2,1},{4,3},{6,5},{9,10},{11,12},{13,14},{10,9},... | collective-permute-start | bytes 49160 | tf_op jit(solution)/shard_map/ppermute | solution.py:629
  2.2 6.6 %collective-permute-start.1 = (f32[4,8,128]{2,1,0:T(8,128)S(1)}, f32[4,8,128]{2,1,0:T(8,128)S(1)}, u32[]{:S(2)}, u32[]{:S(2)}) collective-permute-start(f32[4,8,128]{2,1,0:T(8,128)S(1)} %get-tuple-element.8), channel_id=1, source_target_pairs={{0,1},{2,3},{4,5},{6,7},{1,0},{3,2},{5,4},{7,6},{8,9},{10,11},{12,... | collective-permute-start | bytes 49160 | tf_op jit(solution)/shard_map/ppermute | solution.py:630

commit v6 on v5

--- a/solution.py
+++ b/solution.py
@@ -323,7 +323,59 @@
         behind = [even[k] - odd[k] for k in range(3)]
         return here, ahead, behind
 
-    def sweep(closed, count, load, keep, drive, value, store, root_s, push_s, inverse_s, shear_s):
+    def window_parts(w):
+        zs, zd = [], []
+        for k in range(3):
+            after = pltpu.roll(w[k], depth - 1, 2) * half_last_z
+            before = pltpu.roll(w[k], 1, 2) * half_first_z
+            zs.append(after + before)
+            zd.append(after - before)
+        mean = [w[k] + zs[k] for k in range(2)]
+        mixed = [CROSS2 * w[k] + (2.0 * CROSS3) * zs[k] for k in range(2)]
+        lift = [0.5 * mean[k] + mixed[k] for k in range(2)]
+        strong = [(2.0 * PAIR) * mean[k] + (AXIAL - 2.0 * PAIR) * w[k] for k in range(2)]
+        upright = w[2] + (2.0 * PAIR) * zs[2]
+        flat = FLAT * w[2] + (2.0 * FULL) * zs[2]
+        edge = [(2.0 * CROSS2) * zd[k] for k in range(3)]
+        tip = [(2.0 * CROSS3) * zd[k] for k in range(3)]
+        here = [
+            (zs[0] + zs[0], mean[0], None),
+            (zs[1] + zs[1], strong[1], edge[2]),
+            ((2.0 * AXIAL) * zs[2], upright, edge[1]),
+        ]
+        ahead = [
+            (strong[0] + edge[2], lift[0] + tip[2], mixed[1]),
+            (mean[1], lift[1], tip[2] + mixed[0]),
+            (upright + edge[0], flat + tip[0], tip[1]),
+        ]
+        behind = [
+            (strong[0] - edge[2], lift[0] - tip[2], -mixed[1]),
+            (mean[1], lift[1], tip[2] - mixed[0]),
+            (upright - edge[0], flat - tip[0], tip[1]),
+        ]
+        return tuple([term for row in part for term in row] for part in (here, ahead, behind))
+
+    def window_sums(terms):
+        sums = []
+        for k in range(3):
+            stays, even, odd = terms[3 * k : 3 * k + 3]
+            after = along_y(even + odd, False)[0]
+            before = along_y(even - odd, False)[1]
+            sums.append(stays + after + before)
+        return sums
+
+    def slab_parts(w):
+        return field_parts(w, True)
+
+    def slab_sums(terms):
+        return terms
+
+    def joined(left, right):
+        return [b if a is None else a + b for a, b in zip(left, right)]
+
+    def sweep(
+        parts, sums, count, load, keep, drive, value, store, root_s, push_s, inverse_s, shear_s
+    ):
         offset = (wide - count) // 2
         partial = None
         trail = None
@@ -334,7 +386,7 @@
             if drive is not None:
                 free = 1.0 - value(3, i + offset - 1) * at_bottom
                 r = r * free
-            here, ahead, behind = field_parts([r * load(k, i) for k in range(3)], closed)
+            here, ahead, behind = parts([r * load(k, i) for k in range(3)])
             if i >= 2:
                 j = i - 1
                 d = j + offset - 1
@@ -345,13 +397,14 @@
                     shear[0] * old[0] + shear[2] * old[2],
                     shear[1] * old[0] + shear[2] * old[1],
                 ]
+                total = sums(joined(partial, ahead))
                 for k in range(3):
-                    new = keep * old[k] + (partial[k] + ahead[k] - rest[k]) * inverse_s[k, d]
+                    new = keep * old[k] + (total[k] - rest[k]) * inverse_s[k, d]
                     if drive is not None:
                         new = (new + drive * push_s[k, d]) * held
                     store(k, j - 1, new)
             if i >= 1:
-                partial = [here[k] + trail[k] for k in range(3)]
+                partial = joined(here, trail)
             trail = behind
 
     keep_second = (1.0 - omegas[1]) / omegas[1] + 1.0 / omegas[0]
@@ -374,11 +427,19 @@
                 field_v[k, i - 1, pl.ds(t, SUB, stride=fold), :] = scale * new[t]
 
     arrays = (root_a, push_a, inverse_a, shear_a)
+    whole = (slab_parts, slab_sums)
     sweep(
-        True, wide - 2, lambda k, i: push_a[k, i], keep_second, None, value, store_first_a, *arrays
+        *whole,
+        wide - 2,
+        lambda k, i: push_a[k, i],
+        keep_second,
+        None,
+        value,
+        store_first_a,
+        *arrays,
     )
     sweep(
-        True,
+        *whole,
         wide - 4,
         lambda k, i: first_a[k, i],
         keep_third,
@@ -411,6 +472,8 @@
     def store_second_b(k, i, new):
         second_b[k, i] = new
 
+    window_only = (window_parts, window_sums)
+
     @pl.loop(0, groups)
     def add_case(other):
         @pl.when(other == 0)
@@ -430,7 +493,7 @@
             value = pushes(which, y_of, drive_b, inv_b, inverse_b, push_b)
             arrays = (root_b, push_b, inverse_b, shear_b)
             sweep(
-                False,
+                *window_only,
                 wide - 2,
                 lambda k, i: push_b[k, i],
                 keep_second,
@@ -440,7 +503,7 @@
                 *arrays,
             )
             sweep(
-                False,
+                *window_only,
                 wide - 4,
                 lambda k, i: first_b[k, i],
                 keep_third,
@@ -458,13 +521,14 @@
             w = [r * v[k] for k in range(3)]
             for n, (a, b) in enumerate(((0, 0), (1, 1), (2, 2), (0, 1), (0, 2), (1, 2))):
                 squares_b[n, i] += w[a] * v[b]
-            here, ahead, behind = field_parts(w, False)
+            here, ahead, behind = window_parts(w)
             if i >= 2:
                 old = [second_b[k, i - 1] for k in range(3)]
-                dot = [old[k] * (partial[k] + ahead[k]) for k in range(3)]
+                total = window_sums(joined(partial, ahead))
+                dot = [old[k] * total[k] for k in range(3)]
                 gathered[i - 2] += dot[0] + dot[1] + dot[2]
             if i >= 1:
-                partial = [here[k] + trail[k] for k in range(3)]
+                partial = joined(here, trail)
             trail = behind
 
     def square_parts(q):

time: 25.4 us -> 25.2 us (level)
  no operation moved by 1% of the time
where the time goes in v6:
time: 25.2 us; the launch traced here: 25 us
  blocking collectives  9.28 us (37%)
  Pallas kernels  8.55 us (34%)
  starting transfers between devices  5.11 us (20%)
  between operations  1.99 us (8%)
    all_to_all x1, blocking collectives, shards(): lax.all_to_all(mine, 'case', split_axis=0, concat_axis=0, tiled=True)  9.28 us
    pallas_call x1, Pallas kernels, relaxed(): pl.pallas_call(relax_kernel, out_shape=(jax.ShapeDtypeStruct((3, cells, r...  6.9 us
    ppermute x1, starting transfers between devices, shards(): inner = lax.ppermute(near, 'space', inside)  4.45 us
    pallas_call x1, Pallas kernels, solids(): pl.pallas_call(solid_kernel, out_shape=[pltpu.VMEM((planes, band, depth),...  0.86 us
    pallas_call x1, Pallas kernels, settings(): pl.pallas_call(settings_kernel, out_shape=pltpu.VMEM((1, band, depth), jn...  0.79 us
    ppermute x1, starting transfers between devices, shards(): outer = lax.ppermute(far, 'space', across)  0.66 us
  transfers between devices with their start and end apart: 2, of which 0 were waited for; matrix products, arithmetic and copies ran while one was open for 0% of the time, Pallas kernels for 3%

profile of v6, /device:TPU:0, one launch (start us, length us, event | category | flops | bytes accessed | tf_op | source)
XLA Modules:
  0.0 25.0 jit_solution(9168988858915706719)
XLA Ops:
  0.6 0.9 %shard_map.77 = (f32[6,8,128]{2,1,0:T(8,128)S(1)}, f32[4,8,128]{2,1,0:T(8,128)S(1)}, f32[4,8,128]{2,1,0:T(8,128)S(1)}) custom-call(f32[6,8,128]{2,1,0:T(8,128)} %density_in.1, s32[6,8]{1,0:T(8,128)} %void_in.1), custom_call_target="tpu_custom_call" | custom-call | tf_op jit(solution)/shard_map/pallas_call | solution.py:598
  1.5 0.7 %collective-permute-start = (f32[4,8,128]{2,1,0:T(8,128)S(1)}, f32[4,8,128]{2,1,0:T(8,128)S(1)}, u32[]{:S(2)}, u32[]{:S(2)}) collective-permute-start(f32[4,8,128]{2,1,0:T(8,128)S(1)} %get-tuple-element.7), channel_id=1, source_target_pairs={{1,2},{3,4},{5,6},{2,1},{4,3},{6,5},{9,10},{11,12},{13,14},{10,9},... | collective-permute-start | bytes 49160 | tf_op jit(solution)/shard_map/ppermute | solution.py:693
  2.2 4.5 %collective-permute-start.1 = (f32[4,8,128]{2,1,0:T(8,128)S(1)}, f32[4,8,128]{2,1,0:T(8,128)S(1)}, u32[]{:S(2)}, u32[]{:S(2)}) collective-permute-start(f32[4,8,128]{2,1,0:T(8,128)S(1)} %get-tuple-element.8), channel_id=1, source_target_pairs={{0,1},{2,3},{4,5},{6,7},{1,0},{3,2},{5,4},{7,6},{8,9},{10,11},{12,... | collective-permute-start | bytes 49160 | tf_op jit(solution)/shard_map/ppermute | solution.py:694
  7.9 0.8 %shard_map.78 = f32[1,8,128]{2,1,0:T(8,128)S(1)} custom-call(s32[1,2]{1,0:T(1,128)} %supports_in.1, f32[3,1,48]{2,1,0:T(1,128)} %bitcast.2, s32[1]{0:T(128)S(6)} %copy.8.load_x_ref, s32[1]{0:T(128)S(6)} %copy.9.load_y_ref), custom_call_target="tpu_custom_call" | custom-call | tf_op jit(solution)/shard_map/pallas_call | solution.py:615
  8.7 0.0 collective-permute-done
  8.7 0.0 collective-permute-done.1
  8.8 9.3 %all_to_all.5.bands_ref = f32[4,15,8,128]{3,2,1,0:T(8,128)S(1)} all-to-all(f32[4,15,8,128]{3,2,1,0:T(8,128)S(1)} %broadcast_in_dim.4), channel_id=1, replica_groups=mesh['case'=4,'space'=8] {'case'}, dimensions={0} | all-to-all | bytes 491520 | tf_op jit(solution)/shard_map/all_to_all | solution.py:700
  18.1 6.9 %shard_map.79 = (f32[3,6,32,128]{3,2,1,0:T(8,128)}, f32[6,8,128]{2,1,0:T(8,128)}) custom-call(f32[4,15,8,128]{3,2,1,0:T(8,128)S(1)} %all_to_all.5.bands_ref), custom_call_target="tpu_custom_call" | custom-call | tf_op jit(solution)/shard_map/pallas_call | solution.py:647
  (3 shorter events, 0.0 us)
Async XLA Ops:
  1.5 7.2 %collective-permute-start = (f32[4,8,128]{2,1,0:T(8,128)S(1)}, f32[4,8,128]{2,1,0:T(8,128)S(1)}, u32[]{:S(2)}, u32[]{:S(2)}) collective-permute-start(f32[4,8,128]{2,1,0:T(8,128)S(1)} %get-tuple-element.7), channel_id=1, source_target_pairs={{1,2},{3,4},{5,6},{2,1},{4,3},{6,5},{9,10},{11,12},{13,14},{10,9},... | collective-permute-start | bytes 49160 | tf_op jit(solution)/shard_map/ppermute | solution.py:693
  2.2 6.6 %collective-permute-start.1 = (f32[4,8,128]{2,1,0:T(8,128)S(1)}, f32[4,8,128]{2,1,0:T(8,128)S(1)}, u32[]{:S(2)}, u32[]{:S(2)}) collective-permute-start(f32[4,8,128]{2,1,0:T(8,128)S(1)} %get-tuple-element.8), channel_id=1, source_target_pairs={{0,1},{2,3},{4,5},{6,7},{1,0},{3,2},{5,4},{7,6},{8,9},{10,11},{12,... | collective-permute-start | bytes 49160 | tf_op jit(solution)/shard_map/ppermute | solution.py:694

commit v7 on v6

--- a/solution.py
+++ b/solution.py
@@ -15,6 +15,7 @@
 PATCH = 4.0
 SUB = 8
 CORES = 2
+ABREAST = 3
 HALO = SWEEPS + 1
 EDGE = HALO - 1
 PAD = 8
@@ -459,77 +460,88 @@
     stiffness(fold_b, PAD + top, keep_rows, root_b, drive_b, inv_b, factor_b)
     tensor(False, keep_rows, root_b, shear_b, inverse_b, main_b)
     gathered = work_b.at[pl.ds(wide - 2, cells)]
-    empty = jnp.zeros((fold_b, SUB, depth), jnp.float32)
-    for i in range(cells + 2):
-        for n in range(6):
-            squares_b[n, i] = empty
-    for i in range(cells):
-        gathered[i] = empty
-
-    def store_first_b(k, i, new):
-        first_b[k, i] = new
-
-    def store_second_b(k, i, new):
-        second_b[k, i] = new
-
     window_only = (window_parts, window_sums)
-
-    @pl.loop(0, groups)
-    def add_case(other):
-        @pl.when(other == 0)
-        def take_own():
-            for k in range(3):
-                for i in range(cells + 2):
-                    second_b[k, i] = jnp.stack(
-                        [
-                            third_n[k, i, pl.ds(PAD + top + t, SUB, stride=fold_b), :]
-                            for t in range(fold_b)
-                        ]
-                    )
-
-        @pl.when(other > 0)
-        def relax_other():
-            which = lax.rem(case + other, groups)
-            value = pushes(which, y_of, drive_b, inv_b, inverse_b, push_b)
-            arrays = (root_b, push_b, inverse_b, shear_b)
-            sweep(
-                *window_only,
-                wide - 2,
-                lambda k, i: push_b[k, i],
-                keep_second,
-                None,
-                value,
-                store_first_b,
-                *arrays,
+    products = ((0, 0), (1, 1), (2, 2), (0, 1), (0, 2), (1, 2))
+
+    def relax_other(which, slot):
+        push_s = push_b.at[slot]
+        first_s = first_b.at[slot]
+        value = pushes(which, y_of, drive_b, inv_b, inverse_b, push_s)
+
+        def store_first(k, i, new):
+            first_s[k, i] = new
+
+        def store_second(k, i, new):
+            second_b[slot, k, i] = new
+
+        arrays = (root_b, push_s, inverse_b, shear_b)
+        sweep(
+            *window_only,
+            wide - 2,
+            lambda k, i: push_s[k, i],
+            keep_second,
+            None,
+            value,
+            store_first,
+            *arrays,
+        )
+        sweep(
+            *window_only,
+            wide - 4,
+            lambda k, i: first_s[k, i],
+            keep_third,
+            drive_third,
+            value,
+            store_second,
+            *arrays,
+        )
+
+    def add_energies(places, fresh):
+        for i in range(cells + 2):
+            sums = [None] * len(products)
+            for slot in places:
+                v = [second_b[slot, k, i] for k in range(3)]
+                sums = joined(sums, [v[a] * v[b] for a, b in products])
+            r = root_b[i + EDGE]
+            for n, total in enumerate(sums):
+                if fresh:
+                    squares_b[n, i] = r * total
+                else:
+                    squares_b[n, i] += r * total
+        for slot in places:
+            partial = None
+            trail = None
+            for i in range(cells + 2):
+                r = root_b[i + EDGE]
+                here, ahead, behind = window_parts([r * second_b[slot, k, i] for k in range(3)])
+                if i >= 2:
+                    total = window_sums(joined(partial, ahead))
+                    dot = [second_b[slot, k, i - 1] * total[k] for k in range(3)]
+                    if fresh:
+                        gathered[i - 2] = dot[0] + dot[1] + dot[2]
+                    else:
+                        gathered[i - 2] += dot[0] + dot[1] + dot[2]
+                if i >= 1:
+                    partial = joined(here, trail)
+                trail = behind
+
+    abreast = second_b.shape[0] - 1
+    for k in range(3):
+        for i in range(cells + 2):
+            second_b[abreast, k, i] = jnp.stack(
+                [third_n[k, i, pl.ds(PAD + top + t, SUB, stride=fold_b), :] for t in range(fold_b)]
             )
-            sweep(
-                *window_only,
-                wide - 4,
-                lambda k, i: first_b[k, i],
-                keep_third,
-                drive_third,
-                value,
-                store_second_b,
-                *arrays,
-            )
-
-        partial = None
-        trail = None
-        for i in range(cells + 2):
-            r = root_b[i + EDGE]
-            v = [second_b[k, i] for k in range(3)]
-            w = [r * v[k] for k in range(3)]
-            for n, (a, b) in enumerate(((0, 0), (1, 1), (2, 2), (0, 1), (0, 2), (1, 2))):
-                squares_b[n, i] += w[a] * v[b]
-            here, ahead, behind = window_parts(w)
-            if i >= 2:
-                old = [second_b[k, i - 1] for k in range(3)]
-                total = window_sums(joined(partial, ahead))
-                dot = [old[k] * total[k] for k in range(3)]
-                gathered[i - 2] += dot[0] + dot[1] + dot[2]
-            if i >= 1:
-                partial = joined(here, trail)
-            trail = behind
+    add_energies([abreast], True)
+
+    def add_others(start):
+        for slot in range(abreast):
+            relax_other(lax.rem(case + start + slot, groups), slot)
+        add_energies(range(abreast), False)
+
+    if groups - 1 == abreast:
+        add_others(1)
+    else:
+        pl.loop(1, groups, step=abreast)(add_others)
 
     def square_parts(q):
         qxx, qyy, qzz, qxy, qxz, qyz = q
@@ -637,6 +649,7 @@
     fold = rows // SUB
     fold_b = -(-(band + 2 * HALO) // SUB)
     tall = PAD + rows + fold_b * SUB
+    abreast = ABREAST if (groups - 1) % ABREAST == 0 else 1
 
     def area(*lead):
         return pltpu.VMEM((*lead, fold, SUB, depth), jnp.float32)
@@ -664,13 +677,13 @@
             area(3, wide - 2),
             window(wide),
             window(wide - 2),
+            window(abreast, 3, wide - 2),
             window(3, wide - 2),
             window(3, wide - 2),
-            window(3, wide - 2),
-            window(3, wide - 4),
+            window(abreast, 3, wide - 4),
             window(3, cells),
             window(cells),
-            window(3, cells + 2),
+            window(abreast + 1, 3, cells + 2),
             window(6, cells + 2),
             window(wide - 2 + cells),
             pltpu.VMEM((3, cells, rows, depth), jnp.float32),

time: 25.2 us -> 25.2 us (level)
  no operation moved by 1% of the time
where the time goes in v7:
time: 25.2 us; the launch traced here: 25 us
  blocking collectives  9.28 us (37%)
  Pallas kernels  8.55 us (34%)
  starting transfers between devices  5.11 us (20%)
  between operations  1.99 us (8%)
    all_to_all x1, blocking collectives, shards(): lax.all_to_all(mine, 'case', split_axis=0, concat_axis=0, tiled=True)  9.28 us
    pallas_call x1, Pallas kernels, relaxed(): pl.pallas_call(relax_kernel, out_shape=(jax.ShapeDtypeStruct((3, cells, r...  6.9 us
    ppermute x1, starting transfers between devices, shards(): inner = lax.ppermute(near, 'space', inside)  4.45 us
    pallas_call x1, Pallas kernels, solids(): pl.pallas_call(solid_kernel, out_shape=[pltpu.VMEM((planes, band, depth),...  0.86 us
    pallas_call x1, Pallas kernels, settings(): pl.pallas_call(settings_kernel, out_shape=pltpu.VMEM((1, band, depth), jn...  0.79 us
    ppermute x1, starting transfers between devices, shards(): outer = lax.ppermute(far, 'space', across)  0.66 us
  transfers between devices with their start and end apart: 2, of which 0 were waited for; matrix products, arithmetic and copies ran while one was open for 0% of the time, Pallas kernels for 3%

profile of v7, /device:TPU:0, one launch (start us, length us, event | category | flops | bytes accessed | tf_op | source)
XLA Modules:
  0.0 25.0 jit_solution(18199511169975287023)
XLA Ops:
  0.6 0.9 %shard_map.77 = (f32[6,8,128]{2,1,0:T(8,128)S(1)}, f32[4,8,128]{2,1,0:T(8,128)S(1)}, f32[4,8,128]{2,1,0:T(8,128)S(1)}) custom-call(f32[6,8,128]{2,1,0:T(8,128)} %density_in.1, s32[6,8]{1,0:T(8,128)} %void_in.1), custom_call_target="tpu_custom_call" | custom-call | tf_op jit(solution)/shard_map/pallas_call | solution.py:610
  1.5 0.7 %collective-permute-start = (f32[4,8,128]{2,1,0:T(8,128)S(1)}, f32[4,8,128]{2,1,0:T(8,128)S(1)}, u32[]{:S(2)}, u32[]{:S(2)}) collective-permute-start(f32[4,8,128]{2,1,0:T(8,128)S(1)} %get-tuple-element.7), channel_id=1, source_target_pairs={{1,2},{3,4},{5,6},{2,1},{4,3},{6,5},{9,10},{11,12},{13,14},{10,9},... | collective-permute-start | bytes 49160 | tf_op jit(solution)/shard_map/ppermute | solution.py:706
  2.2 4.5 %collective-permute-start.1 = (f32[4,8,128]{2,1,0:T(8,128)S(1)}, f32[4,8,128]{2,1,0:T(8,128)S(1)}, u32[]{:S(2)}, u32[]{:S(2)}) collective-permute-start(f32[4,8,128]{2,1,0:T(8,128)S(1)} %get-tuple-element.8), channel_id=1, source_target_pairs={{0,1},{2,3},{4,5},{6,7},{1,0},{3,2},{5,4},{7,6},{8,9},{10,11},{12,... | collective-permute-start | bytes 49160 | tf_op jit(solution)/shard_map/ppermute | solution.py:707
  7.9 0.8 %shard_map.78 = f32[1,8,128]{2,1,0:T(8,128)S(1)} custom-call(s32[1,2]{1,0:T(1,128)} %supports_in.1, f32[3,1,48]{2,1,0:T(1,128)} %bitcast.2, s32[1]{0:T(128)S(6)} %copy.8.load_x_ref, s32[1]{0:T(128)S(6)} %copy.9.load_y_ref), custom_call_target="tpu_custom_call" | custom-call | tf_op jit(solution)/shard_map/pallas_call | solution.py:627
  8.7 0.0 collective-permute-done
  8.7 0.0 collective-permute-done.1
  8.8 9.3 %all_to_all.5.bands_ref = f32[4,15,8,128]{3,2,1,0:T(8,128)S(1)} all-to-all(f32[4,15,8,128]{3,2,1,0:T(8,128)S(1)} %broadcast_in_dim.4), channel_id=1, replica_groups=mesh['case'=4,'space'=8] {'case'}, dimensions={0} | all-to-all | bytes 491520 | tf_op jit(solution)/shard_map/all_to_all | solution.py:713
  18.1 6.9 %shard_map.79 = (f32[3,6,32,128]{3,2,1,0:T(8,128)}, f32[6,8,128]{2,1,0:T(8,128)}) custom-call(f32[4,15,8,128]{3,2,1,0:T(8,128)S(1)} %all_to_all.5.bands_ref), custom_call_target="tpu_custom_call" | custom-call | tf_op jit(solution)/shard_map/pallas_call | solution.py:660
  (3 shorter events, 0.0 us)
Async XLA Ops:
  1.5 7.2 %collective-permute-start = (f32[4,8,128]{2,1,0:T(8,128)S(1)}, f32[4,8,128]{2,1,0:T(8,128)S(1)}, u32[]{:S(2)}, u32[]{:S(2)}) collective-permute-start(f32[4,8,128]{2,1,0:T(8,128)S(1)} %get-tuple-element.7), channel_id=1, source_target_pairs={{1,2},{3,4},{5,6},{2,1},{4,3},{6,5},{9,10},{11,12},{13,14},{10,9},... | collective-permute-start | bytes 49160 | tf_op jit(solution)/shard_map/ppermute | solution.py:706
  2.2 6.6 %collective-permute-start.1 = (f32[4,8,128]{2,1,0:T(8,128)S(1)}, f32[4,8,128]{2,1,0:T(8,128)S(1)}, u32[]{:S(2)}, u32[]{:S(2)}) collective-permute-start(f32[4,8,128]{2,1,0:T(8,128)S(1)} %get-tuple-element.8), channel_id=1, source_target_pairs={{0,1},{2,3},{4,5},{6,7},{1,0},{3,2},{5,4},{7,6},{8,9},{10,11},{12,... | collective-permute-start | bytes 49160 | tf_op jit(solution)/shard_map/ppermute | solution.py:707

commit v8 on v7

--- a/solution.py
+++ b/solution.py
@@ -54,7 +54,7 @@
 
 
 def solid_kernel(
-    density_in, void_in, solid_ref, outer_ref, inner_ref, density_ref, void_ref, arrived
+    density_in, void_in, solid_ref, inner_ref, outer_ref, density_ref, void_ref, arrived
 ):
     fetches = [
         pltpu.make_async_copy(void_in, void_ref, arrived.at[0]),
@@ -697,17 +697,18 @@
     cells, band, depth = density.shape
     groups = lax.axis_size("case")
     slabs = lax.axis_size("space")
-    solid, far, near = solids(density, void_depth)
+    solid, near, far = solids(density, void_depth)
     across = [(i, i + 1) for i in range(1, slabs - 1, 2)]
     across += [(j, i) for i, j in across]
     inside = [(i, i + 1) for i in range(0, slabs, 2)]
     inside += [(j, i) for i, j in inside]
     first = lax.rem(lax.axis_index("space"), CORES) == 0
+    inner = lax.ppermute(near, "space", inside)
     outer = lax.ppermute(far, "space", across)
-    inner = lax.ppermute(near, "space", inside)
     row = settings(band, depth, supports, load_x, load_y, load_vectors)
-    before = jnp.where(first, outer, inner)
-    after = jnp.where(first, inner, outer)
+    second = jnp.logical_not(first)
+    before = jnp.where(second, inner, outer)
+    after = jnp.where(second, outer, inner)
     mine = jnp.concatenate([before, solid, after, row])
     mine = jnp.broadcast_to(mine[None], (groups, *mine.shape))
     bands = lax.all_to_all(mine, "case", split_axis=0, concat_axis=0, tiled=True)

time: 25.2 us -> 23.8 us (0.944)
  the two profiles are of different devices: /device:TPU:0 before, /device:TPU:8 now
where the time goes in v8:
time: 23.8 us; the launch traced here: 23.5 us
  blocking collectives  9.97 us (42%)
  Pallas kernels  8.55 us (36%)
  starting transfers between devices  1.99 us (8%)
  between operations  1.98 us (8%)
  waiting for transfers between devices  1.02 us (4%)
    all_to_all x1, blocking collectives, shards(): lax.all_to_all(mine, 'case', split_axis=0, concat_axis=0, tiled=True)  9.97 us
    pallas_call x1, Pallas kernels, relaxed(): pl.pallas_call(relax_kernel, out_shape=(jax.ShapeDtypeStruct((3, cells, r...  6.9 us
    ppermute x1, starting transfers between devices, shards(): outer = lax.ppermute(far, 'space', across)  1.92 us
    ppermute x1, waiting for transfers between devices, shards(): outer = lax.ppermute(far, 'space', across)  1.02 us
    pallas_call x1, Pallas kernels, solids(): pl.pallas_call(solid_kernel, out_shape=[pltpu.VMEM((planes, band, depth),...  0.86 us
    pallas_call x1, Pallas kernels, settings(): pl.pallas_call(settings_kernel, out_shape=pltpu.VMEM((1, band, depth), jn...  0.79 us
  transfers between devices with their start and end apart: 2, of which 1 were waited for; matrix products, arithmetic and copies ran while one was open for 0% of the time, Pallas kernels for 3%

profile of v8, /device:TPU:8, one launch (start us, length us, event | category | flops | bytes accessed | tf_op | source)
XLA Modules:
  0.0 23.5 jit_solution(17041753279657753886)
XLA Ops:
  0.6 0.9 %shard_map.77 = (f32[6,8,128]{2,1,0:T(8,128)S(1)}, f32[4,8,128]{2,1,0:T(8,128)S(1)}, f32[4,8,128]{2,1,0:T(8,128)S(1)}) custom-call(f32[6,8,128]{2,1,0:T(8,128)} %density_in.1, s32[6,8]{1,0:T(8,128)} %void_in.1), custom_call_target="tpu_custom_call" | custom-call | tf_op jit(solution)/shard_map/pallas_call | solution.py:610
  1.5 0.1 collective-permute-start
  1.6 1.9 %collective-permute-start.1 = (f32[4,8,128]{2,1,0:T(8,128)S(1)}, f32[4,8,128]{2,1,0:T(8,128)S(1)}, u32[]{:S(2)}, u32[]{:S(2)}) collective-permute-start(f32[4,8,128]{2,1,0:T(8,128)S(1)} %get-tuple-element.8), channel_id=1, source_target_pairs={{1,2},{3,4},{5,6},{2,1},{4,3},{6,5},{9,10},{11,12},{13,14},{10,9},... | collective-permute-start | bytes 49160 | tf_op jit(solution)/shard_map/ppermute | solution.py:707
  4.8 0.8 %shard_map.78 = f32[1,8,128]{2,1,0:T(8,128)S(1)} custom-call(s32[1,2]{1,0:T(1,128)} %supports_in.1, f32[3,1,48]{2,1,0:T(1,128)} %bitcast.2, s32[1]{0:T(128)S(6)} %copy.8.load_x_ref, s32[1]{0:T(128)S(6)} %copy.9.load_y_ref), custom_call_target="tpu_custom_call" | custom-call | tf_op jit(solution)/shard_map/pallas_call | solution.py:627
  5.6 0.0 collective-permute-done
  5.6 1.0 %collective-permute-done.1 = f32[4,8,128]{2,1,0:T(8,128)S(1)} collective-permute-done((f32[4,8,128]{2,1,0:T(8,128)S(1)}, f32[4,8,128]{2,1,0:T(8,128)S(1)}, u32[]{:S(2)}, u32[]{:S(2)}) %collective-permute-start.1) | collective-permute-done | bytes 16416 | tf_op jit(solution)/shard_map/ppermute | solution.py:707
  6.7 10.0 %all_to_all.5.bands_ref = f32[4,15,8,128]{3,2,1,0:T(8,128)S(1)} all-to-all(f32[4,15,8,128]{3,2,1,0:T(8,128)S(1)} %broadcast_in_dim.4), channel_id=1, replica_groups=mesh['case'=4,'space'=8] {'case'}, dimensions={0} | all-to-all | bytes 491520 | tf_op jit(solution)/shard_map/all_to_all | solution.py:714
  16.6 6.9 %shard_map.79 = (f32[3,6,32,128]{3,2,1,0:T(8,128)}, f32[6,8,128]{2,1,0:T(8,128)}) custom-call(f32[4,15,8,128]{3,2,1,0:T(8,128)S(1)} %all_to_all.5.bands_ref), custom_call_target="tpu_custom_call" | custom-call | tf_op jit(solution)/shard_map/pallas_call | solution.py:660
  (3 shorter events, 0.0 us)
Async XLA Ops:
  1.5 4.1 %collective-permute-start = (f32[4,8,128]{2,1,0:T(8,128)S(1)}, f32[4,8,128]{2,1,0:T(8,128)S(1)}, u32[]{:S(2)}, u32[]{:S(2)}) collective-permute-start(f32[4,8,128]{2,1,0:T(8,128)S(1)} %get-tuple-element.7), channel_id=1, source_target_pairs={{0,1},{2,3},{4,5},{6,7},{1,0},{3,2},{5,4},{7,6},{8,9},{10,11},{12,... | collective-permute-start | bytes 49160 | tf_op jit(solution)/shard_map/ppermute | solution.py:706
  1.6 5.1 %collective-permute-start.1 = (f32[4,8,128]{2,1,0:T(8,128)S(1)}, f32[4,8,128]{2,1,0:T(8,128)S(1)}, u32[]{:S(2)}, u32[]{:S(2)}) collective-permute-start(f32[4,8,128]{2,1,0:T(8,128)S(1)} %get-tuple-element.8), channel_id=1, source_target_pairs={{1,2},{3,4},{5,6},{2,1},{4,3},{6,5},{9,10},{11,12},{13,14},{10,9},... | collective-permute-start | bytes 49160 | tf_op jit(solution)/shard_map/ppermute | solution.py:707

commit v9 on v8

--- a/solution.py
+++ b/solution.py
@@ -291,40 +291,7 @@
                 push_s[k, j] = push * inverse_s[k, j] * value(k, j)
         return value
 
-    def field_parts(w, closed):
-        zs, zd = [], []
-        for k in range(3):
-            after = pltpu.roll(w[k], depth - 1, 2) * half_last_z
-            before = pltpu.roll(w[k], 1, 2) * half_first_z
-            zs.append(after + before)
-            zd.append(after - before)
-        mean = [w[k] + zs[k] for k in range(2)]
-        mixed = [CROSS2 * w[k] + (2.0 * CROSS3) * zs[k] for k in range(2)]
-        even_y = [plus(along_y(0.5 * mean[k] + mixed[k], closed)) for k in range(2)]
-        odd_y = [minus(along_y(mixed[k], closed)) for k in range(2)]
-        strong = [(2.0 * PAIR) * mean[k] + (AXIAL - 2.0 * PAIR) * w[k] for k in range(2)]
-        upright = w[2] + (2.0 * PAIR) * zs[2]
-        flat = FLAT * w[2] + (2.0 * FULL) * zs[2]
-        twist_y = minus(along_y(zd[1], closed))
-        spread_z, twist_z = both(along_y(zd[2], closed))
-        slope_x = (2.0 * CROSS2) * zd[0] + (2.0 * CROSS3) * plus(along_y(zd[0], closed))
-        slope_z = (2.0 * CROSS2) * zd[2] + (2.0 * CROSS3) * spread_z
-        here = [
-            plus(along_y(mean[0], closed)) + (zs[0] + zs[0]),
-            plus(along_y(strong[1], closed)) + (zs[1] + zs[1]) + (2.0 * CROSS2) * twist_z,
-            plus(along_y(upright, closed)) + (2.0 * AXIAL) * zs[2] + (2.0 * CROSS2) * twist_y,
-        ]
-        even = [
-            strong[0] + even_y[0],
-            mean[1] + even_y[1] + (2.0 * CROSS3) * twist_z,
-            upright + plus(along_y(flat, closed)) + (2.0 * CROSS3) * twist_y,
-        ]
-        odd = [odd_y[1] + slope_z, odd_y[0], slope_x]
-        ahead = [even[k] + odd[k] for k in range(3)]
-        behind = [even[k] - odd[k] for k in range(3)]
-        return here, ahead, behind
-
-    def window_parts(w):
+    def field_parts(w):
         zs, zd = [], []
         for k in range(3):
             after = pltpu.roll(w[k], depth - 1, 2) * half_last_z
@@ -356,26 +323,20 @@
         ]
         return tuple([term for row in part for term in row] for part in (here, ahead, behind))
 
-    def window_sums(terms):
+    def field_sums(terms, closed):
         sums = []
         for k in range(3):
             stays, even, odd = terms[3 * k : 3 * k + 3]
-            after = along_y(even + odd, False)[0]
-            before = along_y(even - odd, False)[1]
+            after = along_y(even + odd, closed)[0]
+            before = along_y(even - odd, closed)[1]
             sums.append(stays + after + before)
         return sums
 
-    def slab_parts(w):
-        return field_parts(w, True)
-
-    def slab_sums(terms):
-        return terms
-
     def joined(left, right):
         return [b if a is None else a + b for a, b in zip(left, right)]
 
     def sweep(
-        parts, sums, count, load, keep, drive, value, store, root_s, push_s, inverse_s, shear_s
+        closed, count, load, keep, drive, value, store, root_s, push_s, inverse_s, shear_s
     ):
         offset = (wide - count) // 2
         partial = None
@@ -387,7 +348,7 @@
             if drive is not None:
                 free = 1.0 - value(3, i + offset - 1) * at_bottom
                 r = r * free
-            here, ahead, behind = parts([r * load(k, i) for k in range(3)])
+            here, ahead, behind = field_parts([r * load(k, i) for k in range(3)])
             if i >= 2:
                 j = i - 1
                 d = j + offset - 1
@@ -398,7 +359,7 @@
                     shear[0] * old[0] + shear[2] * old[2],
                     shear[1] * old[0] + shear[2] * old[1],
                 ]
-                total = sums(joined(partial, ahead))
+                total = field_sums(joined(partial, ahead), closed)
                 for k in range(3):
                     new = keep * old[k] + (total[k] - rest[k]) * inverse_s[k, d]
                     if drive is not None:
@@ -428,9 +389,8 @@
                 field_v[k, i - 1, pl.ds(t, SUB, stride=fold), :] = scale * new[t]
 
     arrays = (root_a, push_a, inverse_a, shear_a)
-    whole = (slab_parts, slab_sums)
     sweep(
-        *whole,
+        True,
         wide - 2,
         lambda k, i: push_a[k, i],
         keep_second,
@@ -440,7 +400,7 @@
         *arrays,
     )
     sweep(
-        *whole,
+        True,
         wide - 4,
         lambda k, i: first_a[k, i],
         keep_third,
@@ -460,7 +420,6 @@
     stiffness(fold_b, PAD + top, keep_rows, root_b, drive_b, inv_b, factor_b)
     tensor(False, keep_rows, root_b, shear_b, inverse_b, main_b)
     gathered = work_b.at[pl.ds(wide - 2, cells)]
-    window_only = (window_parts, window_sums)
     products = ((0, 0), (1, 1), (2, 2), (0, 1), (0, 2), (1, 2))
 
     def relax_other(which, slot):
@@ -476,7 +435,7 @@
 
         arrays = (root_b, push_s, inverse_b, shear_b)
         sweep(
-            *window_only,
+            False,
             wide - 2,
             lambda k, i: push_s[k, i],
             keep_second,
@@ -486,7 +445,7 @@
             *arrays,
         )
         sweep(
-            *window_only,
+            False,
             wide - 4,
             lambda k, i: first_s[k, i],
             keep_third,
@@ -513,9 +472,9 @@
             trail = None
             for i in range(cells + 2):
                 r = root_b[i + EDGE]
-                here, ahead, behind = window_parts([r * second_b[slot, k, i] for k in range(3)])
+                here, ahead, behind = field_parts([r * second_b[slot, k, i] for k in range(3)])
                 if i >= 2:
-                    total = window_sums(joined(partial, ahead))
+                    total = field_sums(joined(partial, ahead), False)
                     dot = [second_b[slot, k, i - 1] * total[k] for k in range(3)]
                     if fresh:
                         gathered[i - 2] = dot[0] + dot[1] + dot[2]

time: 23.8 us -> 23.7 us (level)
  no operation moved by 1% of the time
where the time goes in v9:
time: 23.7 us; the launch traced here: 23.4 us
  blocking collectives  9.97 us (42%)
  Pallas kernels  8.45 us (36%)
  starting transfers between devices  1.99 us (8%)
  between operations  1.98 us (8%)
  waiting for transfers between devices  1.02 us (4%)
    all_to_all x1, blocking collectives, shards(): lax.all_to_all(mine, 'case', split_axis=0, concat_axis=0, tiled=True)  9.97 us
    pallas_call x1, Pallas kernels, relaxed(): pl.pallas_call(relax_kernel, out_shape=(jax.ShapeDtypeStruct((3, cells, r...  6.8 us
    ppermute x1, starting transfers between devices, shards(): outer = lax.ppermute(far, 'space', across)  1.92 us
    ppermute x1, waiting for transfers between devices, shards(): outer = lax.ppermute(far, 'space', across)  1.02 us
    pallas_call x1, Pallas kernels, solids(): pl.pallas_call(solid_kernel, out_shape=[pltpu.VMEM((planes, band, depth),...  0.86 us
    pallas_call x1, Pallas kernels, settings(): pl.pallas_call(settings_kernel, out_shape=pltpu.VMEM((1, band, depth), jn...  0.79 us
  transfers between devices with their start and end apart: 2, of which 1 were waited for; matrix products, arithmetic and copies ran while one was open for 0% of the time, Pallas kernels for 3%

profile of v9, /device:TPU:8, one launch (start us, length us, event | category | flops | bytes accessed | tf_op | source)
XLA Modules:
  0.0 23.4 jit_solution(15727243738286314944)
XLA Ops:
  0.6 0.9 %shard_map.77 = (f32[6,8,128]{2,1,0:T(8,128)S(1)}, f32[4,8,128]{2,1,0:T(8,128)S(1)}, f32[4,8,128]{2,1,0:T(8,128)S(1)}) custom-call(f32[6,8,128]{2,1,0:T(8,128)} %density_in.1, s32[6,8]{1,0:T(8,128)} %void_in.1), custom_call_target="tpu_custom_call" | custom-call | tf_op jit(solution)/shard_map/pallas_call | solution.py:569
  1.5 0.1 collective-permute-start
  1.6 1.9 %collective-permute-start.1 = (f32[4,8,128]{2,1,0:T(8,128)S(1)}, f32[4,8,128]{2,1,0:T(8,128)S(1)}, u32[]{:S(2)}, u32[]{:S(2)}) collective-permute-start(f32[4,8,128]{2,1,0:T(8,128)S(1)} %get-tuple-element.8), channel_id=1, source_target_pairs={{1,2},{3,4},{5,6},{2,1},{4,3},{6,5},{9,10},{11,12},{13,14},{10,9},... | collective-permute-start | bytes 49160 | tf_op jit(solution)/shard_map/ppermute | solution.py:666
  4.8 0.8 %shard_map.78 = f32[1,8,128]{2,1,0:T(8,128)S(1)} custom-call(s32[1,2]{1,0:T(1,128)} %supports_in.1, f32[3,1,48]{2,1,0:T(1,128)} %bitcast.2, s32[1]{0:T(128)S(6)} %copy.8.load_x_ref, s32[1]{0:T(128)S(6)} %copy.9.load_y_ref), custom_call_target="tpu_custom_call" | custom-call | tf_op jit(solution)/shard_map/pallas_call | solution.py:586
  5.6 0.0 collective-permute-done
  5.6 1.0 %collective-permute-done.1 = f32[4,8,128]{2,1,0:T(8,128)S(1)} collective-permute-done((f32[4,8,128]{2,1,0:T(8,128)S(1)}, f32[4,8,128]{2,1,0:T(8,128)S(1)}, u32[]{:S(2)}, u32[]{:S(2)}) %collective-permute-start.1) | collective-permute-done | bytes 16416 | tf_op jit(solution)/shard_map/ppermute | solution.py:666
  6.7 10.0 %all_to_all.5.bands_ref = f32[4,15,8,128]{3,2,1,0:T(8,128)S(1)} all-to-all(f32[4,15,8,128]{3,2,1,0:T(8,128)S(1)} %broadcast_in_dim.4), channel_id=1, replica_groups=mesh['case'=4,'space'=8] {'case'}, dimensions={0} | all-to-all | bytes 491520 | tf_op jit(solution)/shard_map/all_to_all | solution.py:673
  16.6 6.8 %shard_map.79 = (f32[3,6,32,128]{3,2,1,0:T(8,128)}, f32[6,8,128]{2,1,0:T(8,128)}) custom-call(f32[4,15,8,128]{3,2,1,0:T(8,128)S(1)} %all_to_all.5.bands_ref), custom_call_target="tpu_custom_call" | custom-call | tf_op jit(solution)/shard_map/pallas_call | solution.py:619
  (3 shorter events, 0.0 us)
Async XLA Ops:
  1.5 4.1 %collective-permute-start = (f32[4,8,128]{2,1,0:T(8,128)S(1)}, f32[4,8,128]{2,1,0:T(8,128)S(1)}, u32[]{:S(2)}, u32[]{:S(2)}) collective-permute-start(f32[4,8,128]{2,1,0:T(8,128)S(1)} %get-tuple-element.7), channel_id=1, source_target_pairs={{0,1},{2,3},{4,5},{6,7},{1,0},{3,2},{5,4},{7,6},{8,9},{10,11},{12,... | collective-permute-start | bytes 49160 | tf_op jit(solution)/shard_map/ppermute | solution.py:665
  1.6 5.1 %collective-permute-start.1 = (f32[4,8,128]{2,1,0:T(8,128)S(1)}, f32[4,8,128]{2,1,0:T(8,128)S(1)}, u32[]{:S(2)}, u32[]{:S(2)}) collective-permute-start(f32[4,8,128]{2,1,0:T(8,128)S(1)} %get-tuple-element.8), channel_id=1, source_target_pairs={{1,2},{3,4},{5,6},{2,1},{4,3},{6,5},{9,10},{11,12},{13,14},{10,9},... | collective-permute-start | bytes 49160 | tf_op jit(solution)/shard_map/ppermute | solution.py:666

commit v10 on v9

--- a/solution.py
+++ b/solution.py
@@ -368,6 +368,11 @@
             if i >= 1:
                 partial = joined(here, trail)
             trail = behind
+            yield
+
+    def together(sweeps):
+        for _ in zip(*sweeps):
+            pass
 
     keep_second = (1.0 - omegas[1]) / omegas[1] + 1.0 / omegas[0]
     keep_third = (1.0 - omegas[2]) / omegas[2]
@@ -389,7 +394,7 @@
                 field_v[k, i - 1, pl.ds(t, SUB, stride=fold), :] = scale * new[t]
 
     arrays = (root_a, push_a, inverse_a, shear_a)
-    sweep(
+    first_sweep = sweep(
         True,
         wide - 2,
         lambda k, i: push_a[k, i],
@@ -399,7 +404,7 @@
         store_first_a,
         *arrays,
     )
-    sweep(
+    second_sweep = sweep(
         True,
         wide - 4,
         lambda k, i: first_a[k, i],
@@ -409,6 +414,8 @@
         store_third_a,
         *arrays,
     )
+    together([first_sweep])
+    together([second_sweep])
     leaving = pltpu.make_async_copy(field_v, field_ref, gone.at[0])
     leaving.start()
 
@@ -422,7 +429,7 @@
     gathered = work_b.at[pl.ds(wide - 2, cells)]
     products = ((0, 0), (1, 1), (2, 2), (0, 1), (0, 2), (1, 2))
 
-    def relax_other(which, slot):
+    def sweeps_other(which, slot):
         push_s = push_b.at[slot]
         first_s = first_b.at[slot]
         value = pushes(which, y_of, drive_b, inv_b, inverse_b, push_s)
@@ -434,7 +441,7 @@
             second_b[slot, k, i] = new
 
         arrays = (root_b, push_s, inverse_b, shear_b)
-        sweep(
+        first_sweep = sweep(
             False,
             wide - 2,
             lambda k, i: push_s[k, i],
@@ -444,7 +451,7 @@
             store_first,
             *arrays,
         )
-        sweep(
+        second_sweep = sweep(
             False,
             wide - 4,
             lambda k, i: first_s[k, i],
@@ -454,6 +461,7 @@
             store_second,
             *arrays,
         )
+        return first_sweep, second_sweep
 
     def add_energies(places, fresh):
         for i in range(cells + 2):
@@ -493,8 +501,11 @@
     add_energies([abreast], True)
 
     def add_others(start):
-        for slot in range(abreast):
-            relax_other(lax.rem(case + start + slot, groups), slot)
+        pairs = [
+            sweeps_other(lax.rem(case + start + slot, groups), slot) for slot in range(abreast)
+        ]
+        for sweeps in zip(*pairs):
+            together(sweeps)
         add_energies(range(abreast), False)
 
     if groups - 1 == abreast:

time: 23.7 us -> 23.7 us (level)
  no operation moved by 1% of the time
where the time goes in v10:
time: 23.7 us; the launch traced here: 23.4 us
  blocking collectives  9.97 us (42%)
  Pallas kernels  8.44 us (36%)
  starting transfers between devices  1.99 us (8%)
  between operations  1.98 us (8%)
  waiting for transfers between devices  1.02 us (4%)
    all_to_all x1, blocking collectives, shards(): lax.all_to_all(mine, 'case', split_axis=0, concat_axis=0, tiled=True)  9.97 us
    pallas_call x1, Pallas kernels, relaxed(): pl.pallas_call(relax_kernel, out_shape=(jax.ShapeDtypeStruct((3, cells, r...  6.79 us
    ppermute x1, starting transfers between devices, shards(): outer = lax.ppermute(far, 'space', across)  1.92 us
    ppermute x1, waiting for transfers between devices, shards(): outer = lax.ppermute(far, 'space', across)  1.02 us
    pallas_call x1, Pallas kernels, solids(): pl.pallas_call(solid_kernel, out_shape=[pltpu.VMEM((planes, band, depth),...  0.86 us
    pallas_call x1, Pallas kernels, settings(): pl.pallas_call(settings_kernel, out_shape=pltpu.VMEM((1, band, depth), jn...  0.79 us
  transfers between devices with their start and end apart: 2, of which 1 were waited for; matrix products, arithmetic and copies ran while one was open for 0% of the time, Pallas kernels for 3%

profile of v10, /device:TPU:8, one launch (start us, length us, event | category | flops | bytes accessed | tf_op | source)
XLA Modules:
  0.0 23.4 jit_solution(16580330110233027557)
XLA Ops:
  0.6 0.9 %shard_map.77 = (f32[6,8,128]{2,1,0:T(8,128)S(1)}, f32[4,8,128]{2,1,0:T(8,128)S(1)}, f32[4,8,128]{2,1,0:T(8,128)S(1)}) custom-call(f32[6,8,128]{2,1,0:T(8,128)} %density_in.1, s32[6,8]{1,0:T(8,128)} %void_in.1), custom_call_target="tpu_custom_call" | custom-call | tf_op jit(solution)/shard_map/pallas_call | solution.py:580
  1.5 0.1 collective-permute-start
  1.6 1.9 %collective-permute-start.1 = (f32[4,8,128]{2,1,0:T(8,128)S(1)}, f32[4,8,128]{2,1,0:T(8,128)S(1)}, u32[]{:S(2)}, u32[]{:S(2)}) collective-permute-start(f32[4,8,128]{2,1,0:T(8,128)S(1)} %get-tuple-element.8), channel_id=1, source_target_pairs={{1,2},{3,4},{5,6},{2,1},{4,3},{6,5},{9,10},{11,12},{13,14},{10,9},... | collective-permute-start | bytes 49160 | tf_op jit(solution)/shard_map/ppermute | solution.py:677
  4.8 0.8 %shard_map.78 = f32[1,8,128]{2,1,0:T(8,128)S(1)} custom-call(s32[1,2]{1,0:T(1,128)} %supports_in.1, f32[3,1,48]{2,1,0:T(1,128)} %bitcast.2, s32[1]{0:T(128)S(6)} %copy.8.load_x_ref, s32[1]{0:T(128)S(6)} %copy.9.load_y_ref), custom_call_target="tpu_custom_call" | custom-call | tf_op jit(solution)/shard_map/pallas_call | solution.py:597
  5.6 0.0 collective-permute-done
  5.6 1.0 %collective-permute-done.1 = f32[4,8,128]{2,1,0:T(8,128)S(1)} collective-permute-done((f32[4,8,128]{2,1,0:T(8,128)S(1)}, f32[4,8,128]{2,1,0:T(8,128)S(1)}, u32[]{:S(2)}, u32[]{:S(2)}) %collective-permute-start.1) | collective-permute-done | bytes 16416 | tf_op jit(solution)/shard_map/ppermute | solution.py:677
  6.7 10.0 %all_to_all.5.bands_ref = f32[4,15,8,128]{3,2,1,0:T(8,128)S(1)} all-to-all(f32[4,15,8,128]{3,2,1,0:T(8,128)S(1)} %broadcast_in_dim.4), channel_id=1, replica_groups=mesh['case'=4,'space'=8] {'case'}, dimensions={0} | all-to-all | bytes 491520 | tf_op jit(solution)/shard_map/all_to_all | solution.py:684
  16.6 6.8 %shard_map.79 = (f32[3,6,32,128]{3,2,1,0:T(8,128)}, f32[6,8,128]{2,1,0:T(8,128)}) custom-call(f32[4,15,8,128]{3,2,1,0:T(8,128)S(1)} %all_to_all.5.bands_ref), custom_call_target="tpu_custom_call" | custom-call | tf_op jit(solution)/shard_map/pallas_call | solution.py:630
  (3 shorter events, 0.0 us)
Async XLA Ops:
  1.5 4.1 %collective-permute-start = (f32[4,8,128]{2,1,0:T(8,128)S(1)}, f32[4,8,128]{2,1,0:T(8,128)S(1)}, u32[]{:S(2)}, u32[]{:S(2)}) collective-permute-start(f32[4,8,128]{2,1,0:T(8,128)S(1)} %get-tuple-element.7), channel_id=1, source_target_pairs={{0,1},{2,3},{4,5},{6,7},{1,0},{3,2},{5,4},{7,6},{8,9},{10,11},{12,... | collective-permute-start | bytes 49160 | tf_op jit(solution)/shard_map/ppermute | solution.py:676
  1.6 5.1 %collective-permute-start.1 = (f32[4,8,128]{2,1,0:T(8,128)S(1)}, f32[4,8,128]{2,1,0:T(8,128)S(1)}, u32[]{:S(2)}, u32[]{:S(2)}) collective-permute-start(f32[4,8,128]{2,1,0:T(8,128)S(1)} %get-tuple-element.8), channel_id=1, source_target_pairs={{1,2},{3,4},{5,6},{2,1},{4,3},{6,5},{9,10},{11,12},{13,14},{10,9},... | collective-permute-start | bytes 49160 | tf_op jit(solution)/shard_map/ppermute | solution.py:677

commit v11 on v10

--- a/solution.py
+++ b/solution.py
@@ -475,22 +475,25 @@
                     squares_b[n, i] = r * total
                 else:
                     squares_b[n, i] += r * total
-        for slot in places:
-            partial = None
-            trail = None
-            for i in range(cells + 2):
-                r = root_b[i + EDGE]
+        partial = [None] * len(places)
+        trail = [None] * len(places)
+        for i in range(cells + 2):
+            r = root_b[i + EDGE]
+            dots = [None]
+            for n, slot in enumerate(places):
                 here, ahead, behind = field_parts([r * second_b[slot, k, i] for k in range(3)])
                 if i >= 2:
-                    total = field_sums(joined(partial, ahead), False)
+                    total = field_sums(joined(partial[n], ahead), False)
                     dot = [second_b[slot, k, i - 1] * total[k] for k in range(3)]
-                    if fresh:
-                        gathered[i - 2] = dot[0] + dot[1] + dot[2]
-                    else:
-                        gathered[i - 2] += dot[0] + dot[1] + dot[2]
+                    dots = joined(dots, [dot[0] + dot[1] + dot[2]])
                 if i >= 1:
-                    partial = joined(here, trail)
-                trail = behind
+                    partial[n] = joined(here, trail[n])
+                trail[n] = behind
+            if i >= 2:
+                if fresh:
+                    gathered[i - 2] = dots[0]
+                else:
+                    gathered[i - 2] += dots[0]
 
     abreast = second_b.shape[0] - 1
     for k in range(3):
@@ -498,20 +501,23 @@
             second_b[abreast, k, i] = jnp.stack(
                 [third_n[k, i, pl.ds(PAD + top + t, SUB, stride=fold_b), :] for t in range(fold_b)]
             )
-    add_energies([abreast], True)
-
-    def add_others(start):
+    def relax_others(start):
         pairs = [
             sweeps_other(lax.rem(case + start + slot, groups), slot) for slot in range(abreast)
         ]
         for sweeps in zip(*pairs):
             together(sweeps)
-        add_energies(range(abreast), False)
 
     if groups - 1 == abreast:
-        add_others(1)
+        relax_others(1)
+        add_energies(range(groups), True)
     else:
-        pl.loop(1, groups, step=abreast)(add_others)
+        add_energies([abreast], True)
+
+        @pl.loop(1, groups, step=abreast)
+        def add_others(start):
+            relax_others(start)
+            add_energies(range(abreast), False)
 
     def square_parts(q):
         qxx, qyy, qzz, qxy, qxz, qyz = q

time: 23.7 us -> 23.7 us (level)
  no operation moved by 1% of the time
where the time goes in v11:
time: 23.7 us; the launch traced here: 23.4 us
  blocking collectives  9.97 us (42%)
  Pallas kernels  8.44 us (36%)
  starting transfers between devices  1.99 us (8%)
  between operations  1.98 us (8%)
  waiting for transfers between devices  1.02 us (4%)
    all_to_all x1, blocking collectives, shards(): lax.all_to_all(mine, 'case', split_axis=0, concat_axis=0, tiled=True)  9.97 us
    pallas_call x1, Pallas kernels, relaxed(): pl.pallas_call(relax_kernel, out_shape=(jax.ShapeDtypeStruct((3, cells, r...  6.78 us
    ppermute x1, starting transfers between devices, shards(): outer = lax.ppermute(far, 'space', across)  1.92 us
    ppermute x1, waiting for transfers between devices, shards(): outer = lax.ppermute(far, 'space', across)  1.02 us
    pallas_call x1, Pallas kernels, solids(): pl.pallas_call(solid_kernel, out_shape=[pltpu.VMEM((planes, band, depth),...  0.86 us
    pallas_call x1, Pallas kernels, settings(): pl.pallas_call(settings_kernel, out_shape=pltpu.VMEM((1, band, depth), jn...  0.79 us
  transfers between devices with their start and end apart: 2, of which 1 were waited for; matrix products, arithmetic and copies ran while one was open for 0% of the time, Pallas kernels for 3%

profile of v11, /device:TPU:8, one launch (start us, length us, event | category | flops | bytes accessed | tf_op | source)
XLA Modules:
  0.0 23.4 jit_solution(1228768188833816398)
XLA Ops:
  0.6 0.9 %shard_map.77 = (f32[6,8,128]{2,1,0:T(8,128)S(1)}, f32[4,8,128]{2,1,0:T(8,128)S(1)}, f32[4,8,128]{2,1,0:T(8,128)S(1)}) custom-call(f32[6,8,128]{2,1,0:T(8,128)} %density_in.1, s32[6,8]{1,0:T(8,128)} %void_in.1), custom_call_target="tpu_custom_call" | custom-call | tf_op jit(solution)/shard_map/pallas_call | solution.py:586
  1.5 0.1 collective-permute-start
  1.6 1.9 %collective-permute-start.1 = (f32[4,8,128]{2,1,0:T(8,128)S(1)}, f32[4,8,128]{2,1,0:T(8,128)S(1)}, u32[]{:S(2)}, u32[]{:S(2)}) collective-permute-start(f32[4,8,128]{2,1,0:T(8,128)S(1)} %get-tuple-element.8), channel_id=1, source_target_pairs={{1,2},{3,4},{5,6},{2,1},{4,3},{6,5},{9,10},{11,12},{13,14},{10,9},... | collective-permute-start | bytes 49160 | tf_op jit(solution)/shard_map/ppermute | solution.py:683
  4.8 0.8 %shard_map.78 = f32[1,8,128]{2,1,0:T(8,128)S(1)} custom-call(s32[1,2]{1,0:T(1,128)} %supports_in.1, f32[3,1,48]{2,1,0:T(1,128)} %bitcast.2, s32[1]{0:T(128)S(6)} %copy.8.load_x_ref, s32[1]{0:T(128)S(6)} %copy.9.load_y_ref), custom_call_target="tpu_custom_call" | custom-call | tf_op jit(solution)/shard_map/pallas_call | solution.py:603
  5.6 0.0 collective-permute-done
  5.6 1.0 %collective-permute-done.1 = f32[4,8,128]{2,1,0:T(8,128)S(1)} collective-permute-done((f32[4,8,128]{2,1,0:T(8,128)S(1)}, f32[4,8,128]{2,1,0:T(8,128)S(1)}, u32[]{:S(2)}, u32[]{:S(2)}) %collective-permute-start.1) | collective-permute-done | bytes 16416 | tf_op jit(solution)/shard_map/ppermute | solution.py:683
  6.7 10.0 %all_to_all.5.bands_ref = f32[4,15,8,128]{3,2,1,0:T(8,128)S(1)} all-to-all(f32[4,15,8,128]{3,2,1,0:T(8,128)S(1)} %broadcast_in_dim.4), channel_id=1, replica_groups=mesh['case'=4,'space'=8] {'case'}, dimensions={0} | all-to-all | bytes 491520 | tf_op jit(solution)/shard_map/all_to_all | solution.py:690
  16.6 6.8 %shard_map.79 = (f32[3,6,32,128]{3,2,1,0:T(8,128)}, f32[6,8,128]{2,1,0:T(8,128)}) custom-call(f32[4,15,8,128]{3,2,1,0:T(8,128)S(1)} %all_to_all.5.bands_ref), custom_call_target="tpu_custom_call" | custom-call | tf_op jit(solution)/shard_map/pallas_call | solution.py:636
  (3 shorter events, 0.0 us)
Async XLA Ops:
  1.5 4.1 %collective-permute-start = (f32[4,8,128]{2,1,0:T(8,128)S(1)}, f32[4,8,128]{2,1,0:T(8,128)S(1)}, u32[]{:S(2)}, u32[]{:S(2)}) collective-permute-start(f32[4,8,128]{2,1,0:T(8,128)S(1)} %get-tuple-element.7), channel_id=1, source_target_pairs={{0,1},{2,3},{4,5},{6,7},{1,0},{3,2},{5,4},{7,6},{8,9},{10,11},{12,... | collective-permute-start | bytes 49160 | tf_op jit(solution)/shard_map/ppermute | solution.py:682
  1.6 5.1 %collective-permute-start.1 = (f32[4,8,128]{2,1,0:T(8,128)S(1)}, f32[4,8,128]{2,1,0:T(8,128)S(1)}, u32[]{:S(2)}, u32[]{:S(2)}) collective-permute-start(f32[4,8,128]{2,1,0:T(8,128)S(1)} %get-tuple-element.8), channel_id=1, source_target_pairs={{1,2},{3,4},{5,6},{2,1},{4,3},{6,5},{9,10},{11,12},{13,14},{10,9},... | collective-permute-start | bytes 49160 | tf_op jit(solution)/shard_map/ppermute | solution.py:683
